TPU v7x, 32 devices: a whole 2x2x4 slice. The times are simulated.
32 devices in a mesh: section: 2 (over core), tensor: 4 (over y, x), dp: 4 (over z).
Axes of the slice: x: 2, y: 2, z: 4, core: 2. Of those that a mesh axis runs over, the one named last changes fastest.
Arguments:
- hidden_in: bfloat16 [2, 512, 1024], P(None, 'dp', 'tensor'), may hold values from -6 to 6
- cotangent: bfloat16 [2, 512, 1024], P(None, 'dp', 'tensor'), may hold values from -6 to 6
- lengths: int32 [2, 8], replicated, may hold values from 1 to 256, as said below
- w_qkv: bfloat16 [2, 1024, 3, 1024], P('section', None, None, 'tensor'), may hold values from -0.1875 to 0.1875
- w_out: bfloat16 [2, 1024, 1024], P('section', 'tensor'), may hold values from -0.1875 to 0.1875
- w_ug: bfloat16 [2, 1024, 2, 4096], P('section', None, None, 'tensor'), may hold values from -0.1875 to 0.1875
- w_down: bfloat16 [2, 4096, 1024], P('section', 'tensor'), may hold values from -0.09375 to 0.09375
- s_qk: float32 [2, 1024], P('section', 'tensor'), may hold values from 0.6 to 1.6
- s_uv: float32 [2, 2, 4096], P('section', None, 'tensor'), may hold values from 0.5 to 2
- alpha: float32 [2, 2, 1024], P('section', None, 'tensor'), may hold values from 0.15 to 0.6
Outputs:
- layer_outputs: bfloat16 [2, 2, 512, 1024], P('section', None, 'dp', 'tensor')
- input_grads: bfloat16 [2, 2, 512, 1024], P('section', None, 'dp', 'tensor')
- grad_w_qkv: float32 [2, 1024, 3, 1024], P('section', 'dp', None, 'tensor')
- grad_w_out: float32 [2, 1024, 1024], P('section', ('tensor', 'dp'))
- grad_w_ug: float32 [2, 1024, 2, 4096], P('section', 'dp', None, 'tensor')
- grad_w_down: float32 [2, 4096, 1024], P('section', ('tensor', 'dp'))
- grad_s_qk: float32 [2, 1024], P('section', ('tensor', 'dp'))
- grad_s_uv: float32 [2, 2, 4096], P('section', None, ('tensor', 'dp'))
- grad_alpha: float32 [2, 2, 1024], P('section', None, ('tensor', 'dp'))
Inputs may be any that keep to these rules, and one draw needn't show every extreme that they name: In each row the 8 lengths sum to 512; the first is exactly 256 and none is longer.
All inputs are finite; a program needn't handle non-finite values.
Results may differ from a plain program's by a relative error of at most 0.038.
Values may be sent and summed in bfloat16 or wider, within the bound.
A program may use at most 128 MiB of HBM per device.

v0:
```python
import math

import jax
import jax.numpy as jnp
from jax import lax
from jax.sharding import PartitionSpec as P

D = 1024
HEAD_DIM = 64
SEQ_CAP = 4096


EPSILON = 1e-05
HIGHEST = lax.Precision.HIGHEST
NEG_LARGE = -1e30


def passed_along(array, axis, by):
    count = lax.axis_size(axis)
    return lax.ppermute(array, axis, [(i, (i + by) % count) for i in range(count)])


def from_behind(array, axis, by):
    count = lax.axis_size(axis)
    pairs = [(i, i + by) for i in range(count) if 0 <= i + by < count]
    return lax.ppermute(array, axis, pairs)


def seq_table(lengths_row, positions):
    seq_end = jnp.cumsum(lengths_row)
    seq_start = seq_end - lengths_row
    segment = jnp.sum((positions[:, None] >= seq_end[None, :]).astype(jnp.int32), axis=1)
    labels = jnp.arange(lengths_row.shape[0], dtype=jnp.int32)
    first_tok = jnp.sum(
        jnp.where(segment[:, None] == labels[None, :], seq_start[None, :], 0), axis=1
    )
    return (segment, positions - first_tok)


def rope_tables(places, col_width):
    column = jnp.arange(col_width, dtype=jnp.int32) % HEAD_DIM
    half_dim = HEAD_DIM // 2
    rope_rates = 10000.0 ** (-(column % half_dim).astype(jnp.float32) / half_dim)
    angles = places.astype(jnp.float32)[:, None] * rope_rates[None, :]
    return (jnp.cos(angles), jnp.sin(angles), column < half_dim)


def partner(values, lower_half):
    half_dim = HEAD_DIM // 2
    return jnp.where(
        lower_half[None, :],
        -jnp.roll(values, -half_dim, axis=1),
        jnp.roll(values, half_dim, axis=1),
    )


def contract_rows(left_op, right_op):
    return lax.dot_general(
        left_op, right_op, (((0,), (0,)), ((), ())), preferred_element_type=jnp.float32
    )


def contract_cols(left_op, right_op):
    return lax.dot_general(
        left_op, right_op, (((1,), (1,)), ((), ())), preferred_element_type=jnp.float32
    )


def full_rows(columns):
    return lax.all_gather(columns, "tensor", axis=1, tiled=True)


def to_cols(partial_sum):
    return lax.psum_scatter(
        partial_sum.astype(jnp.bfloat16), "tensor", scatter_dimension=1, tiled=True
    ).astype(jnp.float32)


def grad_rows(columns):
    return lax.all_gather(columns, "tensor", axis=1, tiled=True)


def grad_cols(partial_sum):
    return lax.psum_scatter(
        partial_sum.astype(jnp.bfloat16), "tensor", scatter_dimension=1, tiled=True
    ).astype(jnp.float32)


def row_total(values):
    return lax.psum(jnp.sum(values, axis=1), "tensor")


def sphere(values):
    row_ratio = lax.rsqrt(row_total(values * values) / D + EPSILON)[:, None]
    return (values * row_ratio, row_ratio)


def sphere_back(source, row_ratio, grad_in):
    inner_sum = row_total(grad_in * source)[:, None]
    return row_ratio * grad_in - source * (row_ratio * row_ratio * row_ratio) * inner_sum / D


def pass_on(dkv_sum):
    return passed_along(dkv_sum.astype(jnp.bfloat16), "dp", 1).astype(dkv_sum.dtype)


def unchanged(previous):
    return previous


def per_device(hidden_in, cotangent, lengths, w_qkv, w_out, w_ug, w_down, s_qk, s_uv, alpha):
    micro_n = hidden_in.shape[0]
    tok_rows = hidden_in.shape[1]
    col_width = hidden_in.shape[2]
    heads_here = col_width // HEAD_DIM
    ff_here = w_down.shape[1]
    dp_ranks = lax.axis_size("dp")
    dp_rank = lax.axis_index("dp")
    longest = min(SEQ_CAP, tok_rows * dp_ranks // 2)
    reach_len = min(dp_ranks - 1, (longest + tok_rows - 2) // tok_rows)
    first_section = lax.axis_index("section") == 0
    score_div = math.sqrt(HEAD_DIM)
    qkv_mat = w_qkv[0].reshape(D, 3 * col_width)
    out_mat = w_out[0]
    ug_mat = w_ug[0].reshape(D, 2 * ff_here)
    down_mat = w_down[0]
    scale_qk = s_qk[0]
    scale_up = s_uv[0, 0]
    scale_gate = s_uv[0, 1]
    alpha_attn = alpha[0, 0]
    alpha_mlp = alpha[0, 1]
    local_rows = jnp.arange(tok_rows, dtype=jnp.int32)
    q_index = dp_rank * tok_rows + local_rows
    indicator = (
        jnp.arange(col_width, dtype=jnp.int32)[:, None] // HEAD_DIM
        == jnp.arange(heads_here, dtype=jnp.int32)[None, :]
    ).astype(jnp.float32)

    def head_sum(values):
        return jnp.dot(values, indicator, precision=HIGHEST, preferred_element_type=jnp.float32)

    def spread(small):
        return jnp.dot(small, indicator.T, precision=HIGHEST, preferred_element_type=jnp.float32)

    def block_info(lengths_row, q_segment, offset):
        source = dp_rank - offset
        k_index = source * tok_rows + local_rows
        k_segment, unused = seq_table(lengths_row, k_index)
        key_mask = (
            (k_segment[None, :] == q_segment[:, None])
            & (k_index[None, :] <= q_index[:, None])
            & (k_index[None, :] >= 0)
        )
        needed = (source * tok_rows + tok_rows - 1 >= 0) & (k_segment[tok_rows - 1] >= q_segment[0])
        return (key_mask, needed)

    def block_scores(q_heads, kv_block):
        key_heads = kv_block[:, :col_width].reshape(tok_rows, heads_here, HEAD_DIM)
        return (
            jnp.einsum("qhd,khd->hqk", q_heads, key_heads, preferred_element_type=jnp.float32)
            / score_div
        )

    def prep_back(grad_n, rotated, head_ratio, record):
        unit_vec = rotated * head_ratio
        d_scale = jnp.sum(grad_n * unit_vec, axis=0)
        d_unit = grad_n * scale_qk[None, :]
        d_rot = head_ratio * d_unit - rotated * (head_ratio * head_ratio * head_ratio) * spread(
            head_sum(d_unit * rotated) / HEAD_DIM
        )
        return (
            d_rot * record["cosine"] - partner(d_rot * record["sine_tab"], record["lower_half"]),
            d_scale,
        )

    received_in = jnp.zeros((tok_rows, col_width), jnp.bfloat16)
    records = []
    results = []
    for tick_no in range(micro_n + 1):
        early_mb = min(tick_no, micro_n - 1)
        late_mb = max(tick_no - 1, 0)
        lengths_row = jnp.where(first_section, lengths[early_mb], lengths[late_mb])
        layer_in = jnp.where(first_section, hidden_in[early_mb], received_in)
        hidden = layer_in.astype(jnp.float32)
        forward_q_segment, places = seq_table(lengths_row, q_index)
        cosine, sine_tab, lower_half = rope_tables(places, col_width)
        full_in = full_rows(hidden.astype(jnp.bfloat16))
        qkv = jnp.dot(full_in, qkv_mat, preferred_element_type=jnp.float32)
        q_raw = qkv[:, :col_width]
        k_raw = qkv[:, col_width : 2 * col_width]
        q_rot = q_raw * cosine + partner(q_raw, lower_half) * sine_tab
        k_rot = k_raw * cosine + partner(k_raw, lower_half) * sine_tab
        q_ratio = spread(lax.rsqrt(head_sum(q_rot * q_rot) / HEAD_DIM + EPSILON))
        k_ratio = spread(lax.rsqrt(head_sum(k_rot * k_rot) / HEAD_DIM + EPSILON))
        query_b = (q_rot * q_ratio * scale_qk[None, :]).astype(jnp.bfloat16)
        key_b = (k_rot * k_ratio * scale_qk[None, :]).astype(jnp.bfloat16)
        value_b = qkv[:, 2 * col_width :].astype(jnp.bfloat16)
        forward_q_heads = query_b.reshape(tok_rows, heads_here, HEAD_DIM)
        own_block = jnp.concatenate([key_b, value_b], axis=1)

        def lse_step(lse_state, kv_block, offset):
            key_mask, needed = block_info(lengths_row, forward_q_segment, offset)

            def update(previous):
                run_max, run_sum = previous
                masked = jnp.where(
                    key_mask[None], block_scores(forward_q_heads, kv_block), NEG_LARGE
                )
                new_max = jnp.maximum(run_max, jnp.max(masked, axis=2))
                exp_terms = jnp.where(key_mask[None], jnp.exp(masked - new_max[:, :, None]), 0.0)
                return (new_max, run_sum * jnp.exp(run_max - new_max) + jnp.sum(exp_terms, axis=2))

            return lax.cond(needed, update, unchanged, lse_state)

        init_state = (
            jnp.full((heads_here, tok_rows), NEG_LARGE, jnp.float32),
            jnp.zeros((heads_here, tok_rows), jnp.float32),
        )
        lse_state = lse_step(init_state, own_block, jnp.int32(0))

        def cycle_step(state_in, offset):
            kv_block, lse_now = state_in
            kv_block = from_behind(kv_block, "dp", 1)
            return ((kv_block, lse_step(lse_now, kv_block, offset)), kv_block)

        (forward_unused_block, lse_state), received = lax.scan(
            cycle_step, (own_block, lse_state), jnp.arange(1, reach_len + 1, dtype=jnp.int32)
        )
        kv_stack = jnp.concatenate([own_block[None], received], axis=0)
        forward_log_total = lse_state[0] + jnp.log(lse_state[1])

        def value_step(acc_heads, scan_item):
            kv_block, offset = scan_item
            key_mask, needed = block_info(lengths_row, forward_q_segment, offset)

            def add_values(previous):
                attn_prob = jnp.where(
                    key_mask[None],
                    jnp.exp(
                        block_scores(forward_q_heads, kv_block) - forward_log_total[:, :, None]
                    ),
                    0.0,
                ).astype(jnp.bfloat16)
                val_heads = kv_block[:, col_width:].reshape(tok_rows, heads_here, HEAD_DIM)
                return previous + jnp.einsum(
                    "hqk,khd->hqd", attn_prob, val_heads, preferred_element_type=jnp.float32
                )

            return (lax.cond(needed, add_values, unchanged, acc_heads), None)

        acc_heads, forward_unused_out = lax.scan(
            value_step,
            jnp.zeros((heads_here, tok_rows, HEAD_DIM), jnp.float32),
            (kv_stack, jnp.arange(reach_len + 1, dtype=jnp.int32)),
        )
        attended = jnp.transpose(acc_heads, (1, 0, 2)).reshape(tok_rows, col_width)
        attended_b = attended.astype(jnp.bfloat16)
        attn_raw = to_cols(jnp.dot(attended_b, out_mat, preferred_element_type=jnp.float32))
        attn_n, ratio_a = sphere(attn_raw)
        mix_one = hidden + alpha_attn[None, :] * (attn_n - hidden)
        normed_one, ratio_one = sphere(mix_one)
        inner_full = full_rows(normed_one.astype(jnp.bfloat16))
        forward_upgate = jnp.dot(inner_full, ug_mat, preferred_element_type=jnp.float32)
        forward_up_s = forward_upgate[:, :ff_here] * scale_up[None, :]
        forward_gate_s = forward_upgate[:, ff_here:] * scale_gate[None, :]
        act_b = (forward_up_s * jax.nn.silu(forward_gate_s)).astype(jnp.bfloat16)
        mlp_raw = to_cols(jnp.dot(act_b, down_mat, preferred_element_type=jnp.float32))
        mlp_n, ratio_m = sphere(mlp_raw)
        mix_two = normed_one + alpha_mlp[None, :] * (mlp_n - normed_one)
        result, ratio_two = sphere(mix_two)
        kept_blocks = own_block[None]
        forward_record = {
            "lengths_row": lengths_row,
            "q_segment": forward_q_segment,
            "cosine": cosine,
            "sine_tab": sine_tab,
            "lower_half": lower_half,
            "full_in": full_in,
            "q_rot": q_rot,
            "k_rot": k_rot,
            "q_ratio": q_ratio,
            "k_ratio": k_ratio,
            "query_b": query_b,
            "blocks": kept_blocks,
            "log_total": forward_log_total,
            "attended": attended,
            "attended_b": attended_b,
            "hidden": hidden,
            "attn_raw": attn_raw,
            "ratio_a": ratio_a,
            "attn_n": attn_n,
            "mix_one": mix_one,
            "ratio_one": ratio_one,
            "normed_one": normed_one,
            "inner_full": inner_full,
            "upgate": forward_upgate,
            "act_b": act_b,
            "mlp_raw": mlp_raw,
            "ratio_m": ratio_m,
            "mlp_n": mlp_n,
            "mix_two": mix_two,
            "ratio_two": ratio_two,
        }
        record, result = (forward_record, result)
        result_b = result.astype(jnp.bfloat16)
        records.append(record)
        results.append(result_b)
        if tick_no < micro_n:
            received_in = from_behind(result_b, "section", 1)
    layer_outputs = jnp.stack(
        [
            jnp.where(first_section, results[number], results[number + 1])
            for number in range(micro_n)
        ]
    )
    back_in = jnp.zeros((tok_rows, col_width), jnp.bfloat16)
    grad_totals = None
    back_results = []
    for tick_no in range(micro_n + 1):
        record = records[micro_n - tick_no]
        late_cot = cotangent[max(micro_n - 1 - tick_no, 0)].astype(jnp.float32)
        live_flag = jnp.where(
            first_section, 1.0 if tick_no >= 1 else 0.0, 1.0 if tick_no < micro_n else 0.0
        )
        grad_out = jnp.where(first_section, back_in.astype(jnp.float32), late_cot) * live_flag
        backward_lengths_row = record["lengths_row"]
        backward_q_segment = record["q_segment"]
        dz_two = sphere_back(record["mix_two"], record["ratio_two"], grad_out)
        d_normed = (1.0 - alpha_mlp)[None, :] * dz_two
        d_mlp_n = alpha_mlp[None, :] * dz_two
        d_alpha_mlp = jnp.sum(dz_two * (record["mlp_n"] - record["normed_one"]), axis=0)
        d_mlp = sphere_back(record["mlp_raw"], record["ratio_m"], d_mlp_n)
        d_mlp_full = grad_rows(d_mlp.astype(jnp.bfloat16))
        dw_down = contract_rows(record["act_b"], d_mlp_full)
        d_act = contract_cols(d_mlp_full, down_mat)
        upgate = record["upgate"]
        up_s = upgate[:, :ff_here] * scale_up[None, :]
        gate_s = upgate[:, ff_here:] * scale_gate[None, :]
        gate_sig = jax.nn.sigmoid(gate_s)
        d_up = d_act * gate_s * gate_sig
        d_gate = d_act * up_s * gate_sig * (1.0 + gate_s * (1.0 - gate_sig))
        d_scale_up = jnp.sum(d_up * upgate[:, :ff_here], axis=0)
        d_scale_gate = jnp.sum(d_gate * upgate[:, ff_here:], axis=0)
        d_upgate = jnp.concatenate(
            [d_up * scale_up[None, :], d_gate * scale_gate[None, :]], axis=1
        ).astype(jnp.bfloat16)
        dw_ug = contract_rows(record["inner_full"], d_upgate)
        d_normed = d_normed + grad_cols(contract_cols(d_upgate, ug_mat))
        dz_one = sphere_back(record["mix_one"], record["ratio_one"], d_normed)
        d_hidden = (1.0 - alpha_attn)[None, :] * dz_one
        d_attn_n = alpha_attn[None, :] * dz_one
        d_alpha_attn = jnp.sum(dz_one * (record["attn_n"] - record["hidden"]), axis=0)
        d_attn = sphere_back(record["attn_raw"], record["ratio_a"], d_attn_n)
        d_attn_full = grad_rows(d_attn.astype(jnp.bfloat16))
        dw_out = contract_rows(record["attended_b"], d_attn_full)
        d_attended = contract_cols(d_attn_full, out_mat).astype(jnp.bfloat16)
        row_delta = jnp.transpose(head_sum(d_attended.astype(jnp.float32) * record["attended"]))
        do_heads = d_attended.reshape(tok_rows, heads_here, HEAD_DIM)
        backward_q_heads = record["query_b"].reshape(tok_rows, heads_here, HEAD_DIM)
        log_total = record["log_total"]

        def block_grads(dq_now, kv_block, offset):
            key_mask, needed = block_info(backward_lengths_row, backward_q_segment, offset)

            def compute(previous):
                key_heads = kv_block[:, :col_width].reshape(tok_rows, heads_here, HEAD_DIM)
                val_heads = kv_block[:, col_width:].reshape(tok_rows, heads_here, HEAD_DIM)
                attn_prob = jnp.where(
                    key_mask[None],
                    jnp.exp(block_scores(backward_q_heads, kv_block) - log_total[:, :, None]),
                    0.0,
                )
                d_prob = jnp.einsum(
                    "qhd,khd->hqk", do_heads, val_heads, preferred_element_type=jnp.float32
                )
                d_val = jnp.einsum(
                    "hqk,qhd->khd",
                    attn_prob.astype(jnp.bfloat16),
                    do_heads,
                    preferred_element_type=jnp.float32,
                )
                d_score = (attn_prob * (d_prob - row_delta[:, :, None])).astype(jnp.bfloat16)
                new_dq = (
                    previous
                    + jnp.einsum(
                        "hqk,khd->hqd", d_score, key_heads, preferred_element_type=jnp.float32
                    )
                    / score_div
                )
                d_key = (
                    jnp.einsum(
                        "hqk,qhd->khd",
                        d_score,
                        backward_q_heads,
                        preferred_element_type=jnp.float32,
                    )
                    / score_div
                )
                return (
                    jnp.concatenate(
                        [d_key.reshape(tok_rows, col_width), d_val.reshape(tok_rows, col_width)],
                        axis=1,
                    ),
                    new_dq,
                )

            def skipped(previous):
                return (jnp.zeros((tok_rows, 2 * col_width), jnp.float32), previous)

            return lax.cond(needed, compute, skipped, dq_now)

        own_part, dq_acc = block_grads(
            jnp.zeros((heads_here, tok_rows, HEAD_DIM), jnp.float32),
            record["blocks"][0],
            jnp.int32(0),
        )
        offsets = jnp.arange(1, reach_len + 1, dtype=jnp.int32)

        def again_step(state_in, offset):
            dkv_sum, kv_block, dq_now = state_in
            dkv_sum = pass_on(dkv_sum)
            kv_block = from_behind(kv_block, "dp", 1)
            dkv_part, dq_now = block_grads(dq_now, kv_block, offset)
            return ((dkv_sum + dkv_part, kv_block, dq_now), None)

        (dkv_sum, unused_block, dq_acc), unused_out = lax.scan(
            again_step, (own_part, record["blocks"][0], dq_acc), offsets
        )
        dkv_home = passed_along(dkv_sum.astype(jnp.bfloat16), "dp", -reach_len).astype(
            dkv_sum.dtype
        )
        dq_full = jnp.transpose(dq_acc, (1, 0, 2)).reshape(tok_rows, col_width)
        dq_raw, ds_query = prep_back(dq_full, record["q_rot"], record["q_ratio"], record)
        dk_raw, ds_key = prep_back(
            dkv_home[:, :col_width], record["k_rot"], record["k_ratio"], record
        )
        d_qkv = jnp.concatenate([dq_raw, dk_raw, dkv_home[:, col_width:]], axis=1).astype(
            jnp.bfloat16
        )
        dw_qkv = contract_rows(record["full_in"], d_qkv)
        d_hidden = d_hidden + grad_cols(contract_cols(d_qkv, qkv_mat))
        grads = (
            dw_qkv.reshape(D, 3, col_width),
            dw_out,
            dw_ug.reshape(D, 2, ff_here),
            dw_down,
            ds_query + ds_key,
            jnp.stack([d_scale_up, d_scale_gate]),
            jnp.stack([d_alpha_attn, d_alpha_mlp]),
        )
        d_hidden, grads = (d_hidden, grads)
        grad_b = d_hidden.astype(jnp.bfloat16)
        back_results.append(grad_b)
        grad_totals = grads if grad_totals is None else jax.tree.map(jnp.add, grad_totals, grads)
        if tick_no < micro_n:
            back_in = from_behind(grad_b, "section", -1)
    input_grads = jnp.stack(
        [
            jnp.where(
                first_section, back_results[micro_n - number], back_results[micro_n - 1 - number]
            )
            for number in range(micro_n)
        ]
    )
    summed = (
        lax.psum_scatter(
            grad_totals[0].astype(jnp.bfloat16), "dp", scatter_dimension=0, tiled=True
        ).astype(jnp.float32),
        lax.psum_scatter(
            grad_totals[1].astype(jnp.bfloat16), "dp", scatter_dimension=0, tiled=True
        ).astype(jnp.float32),
        lax.psum_scatter(
            grad_totals[2].astype(jnp.bfloat16), "dp", scatter_dimension=0, tiled=True
        ).astype(jnp.float32),
        lax.psum_scatter(
            grad_totals[3].astype(jnp.bfloat16), "dp", scatter_dimension=0, tiled=True
        ).astype(jnp.float32),
        lax.psum_scatter(
            grad_totals[4].astype(jnp.bfloat16), "dp", scatter_dimension=0, tiled=True
        ).astype(jnp.float32),
        lax.psum_scatter(
            grad_totals[5].astype(jnp.bfloat16), "dp", scatter_dimension=1, tiled=True
        ).astype(jnp.float32),
        lax.psum_scatter(
            grad_totals[6].astype(jnp.bfloat16), "dp", scatter_dimension=1, tiled=True
        ).astype(jnp.float32),
    )
    return (
        layer_outputs[None],
        input_grads[None],
        summed[0][None],
        summed[1][None],
        summed[2][None],
        summed[3][None],
        summed[4][None],
        summed[5][None],
        summed[6][None],
    )


def solution(mesh):
    placed = (
        P(None, "dp", "tensor"),
        P(None, "dp", "tensor"),
        P(),
        P("section", None, None, "tensor"),
        P("section", "tensor", None),
        P("section", None, None, "tensor"),
        P("section", "tensor", None),
        P("section", "tensor"),
        P("section", None, "tensor"),
        P("section", None, "tensor"),
    )
    return jax.shard_map(
        per_device,
        mesh=mesh,
        in_specs=placed,
        out_specs=(
            P("section", None, "dp", "tensor"),
            P("section", None, "dp", "tensor"),
            P("section", "dp", None, "tensor"),
            P("section", ("tensor", "dp"), None),
            P("section", "dp", None, "tensor"),
            P("section", ("tensor", "dp"), None),
            P("section", ("tensor", "dp")),
            P("section", None, ("tensor", "dp")),
            P("section", None, ("tensor", "dp")),
        ),
        check_vma=False,
    )
```

profile of v0, /device:TPU:8, one launch (start us, length us, event | category | flops | bytes accessed | tf_op | source)
XLA Modules:
  0.0 1284.9 jit_solution(938854914745005778)
XLA Ops:
  11.8 10.0 all-gather
  41.9 16.3 %while.192 = (s32[]{:T(128)}, bf16[128,512]{0,1:T(8,128)(2,1)S(1)}, f32[4,128]{1,0:T(4,128)}, f32[4,128]{1,0:T(4,128)S(1)}, bf16[2,128,512]{1,2,0:T(8,128)(2,1)S...) while((s32[]{:T(128)}, bf16[128,512]{0,1:T(8,128)(2,1)S(1)}, ...), condition=%wide.region_14.15_spmd.clone.clone, body=%wide.region_8.14_spmd.clone.clone.sunk | while | flops 8851849 | bytes 1917623 | solution.py:226
  74.9 18.6 %reduce-scatter.22.cloned.1.call-done = bf16[128,256]{1,0:T(8,128)(2,1)} async-done(((bf16[128,1024]{1,0:T(8,128)(2,1)}), bf16[128,256]{1,0:T(8,128)(2,1)}) %reduce-scatter.22.cloned.1.call-update) | async-done | bytes 65552 | tf_op jit(solution)/shard_map/reduce_scatter | solution.py:74
  132.0 22.7 %reduce-scatter.24.cloned.1.call-done = bf16[128,256]{1,0:T(8,128)(2,1)} async-done(((bf16[128,1024]{1,0:T(8,128)(2,1)}), bf16[128,256]{1,0:T(8,128)(2,1)}) %reduce-scatter.24.cloned.1.call-update) | async-done | bytes 65552 | tf_op jit(solution)/shard_map/reduce_scatter | solution.py:74
  205.8 20.6 %while.194 = (s32[]{:T(128)}, bf16[128,512]{0,1:T(8,128)(2,1)}, f32[4,128]{1,0:T(4,128)}, f32[4,128]{1,0:T(4,128)S(1)}, bf16[2,128,512]{1,2,0:T(8,128)(2,1)}, /*...) while((s32[]{:T(128)}, bf16[128,512]{0,1:T(8,128)(2,1)}, ...), condition=%wide.region_44.45_spmd.clone.clone, body=%wide.region_38.44_spmd.clone.clone.sunk | while | flops 8851849 | bytes 1917623 | solution.py:226
  228.9 16.3 %while.195 = (s32[]{:T(128)}, f32[4,128,64]{1,2,0:T(8,128)S(1)}, s32[3]{0:T(128)S(1)}, s32[]{:T(128)}, s32[1,8]{1,0:T(1,128)}, /*index=5*/s32[128]{0:T(128)}, bf...) while((s32[]{:T(128)}, f32[4,128,64]{1,2,0:T(8,128)S(1)}, ...), condition=%wide.region_49.50_spmd.clone.clone, body=%wide.region_45.49_spmd.clone.clone.sunk | while | flops 17141128 | bytes 1024623 | solution.py:251
  246.3 22.3 %reduce-scatter.26.cloned.1.call-done = bf16[128,256]{1,0:T(8,128)(2,1)} async-done(((bf16[128,1024]{1,0:T(8,128)(2,1)}), bf16[128,256]{1,0:T(8,128)(2,1)}) %reduce-scatter.26.cloned.1.call-update) | async-done | bytes 65552 | tf_op jit(solution)/shard_map/reduce_scatter | solution.py:74
  305.9 24.1 %reduce-scatter.28.cloned.1.call-done = bf16[128,256]{1,0:T(8,128)(2,1)} async-done(((bf16[128,1024]{1,0:T(8,128)(2,1)}), bf16[128,256]{1,0:T(8,128)(2,1)}) %reduce-scatter.28.cloned.1.call-update) | async-done | bytes 65552 | tf_op jit(solution)/shard_map/reduce_scatter | solution.py:74
  379.7 21.7 %while.196 = (s32[]{:T(128)}, bf16[128,512]{0,1:T(8,128)(2,1)}, f32[4,128]{1,0:T(4,128)}, f32[4,128]{1,0:T(4,128)}, bf16[2,128,512]{1,2,0:T(8,128)(2,1)}, /*inde...) while((s32[]{:T(128)}, bf16[128,512]{0,1:T(8,128)(2,1)}, ...), condition=%wide.region_74.75_spmd.clone.clone, body=%wide.region_68.74_spmd.clone.clone.sunk | while | flops 8851849 | bytes 1917623 | solution.py:226
  403.9 16.1 %while.197 = (s32[]{:T(128)}, f32[4,128,64]{1,2,0:T(8,128)S(1)}, s32[3]{0:T(128)S(1)}, s32[]{:T(128)}, s32[1,8]{1,0:T(1,128)}, /*index=5*/s32[128]{0:T(128)}, bf...) while((s32[]{:T(128)}, f32[4,128,64]{1,2,0:T(8,128)S(1)}, ...), condition=%wide.region_79.80_spmd.clone.clone, body=%wide.region_75.79_spmd.clone.clone.sunk | while | flops 17141128 | bytes 1024623 | solution.py:251
  421.1 22.4 %reduce-scatter.30.cloned.1.call-done = bf16[128,256]{1,0:T(8,128)(2,1)} async-done(((bf16[128,1024]{1,0:T(8,128)(2,1)}), bf16[128,256]{1,0:T(8,128)(2,1)}) %reduce-scatter.30.cloned.1.call-update) | async-done | bytes 65552 | tf_op jit(solution)/shard_map/reduce_scatter | solution.py:74
  481.8 24.1 %reduce-scatter.32.cloned.1.call-done = bf16[128,256]{1,0:T(8,128)(2,1)} async-done(((bf16[128,1024]{1,0:T(8,128)(2,1)}), bf16[128,256]{1,0:T(8,128)(2,1)}) %reduce-scatter.32.cloned.1.call-update) | async-done | bytes 65552 | tf_op jit(solution)/shard_map/reduce_scatter | solution.py:74
  554.7 22.2 %reduce-scatter.34.cloned.1.call-done = bf16[128,256]{1,0:T(8,128)(2,1)} async-done(((bf16[128,1024]{1,0:T(8,128)(2,1)}), bf16[128,256]{1,0:T(8,128)(2,1)}) %reduce-scatter.34.cloned.1.call-update) | async-done | bytes 65552 | tf_op jit(solution)/shard_map/reduce_scatter | solution.py:84
  614.0 26.6 %while.198 = (s32[]{:T(128)}, bf16[128,512]{0,1:T(8,128)(2,1)}, bf16[128,512]{0,1:T(8,128)(2,1)}, f32[4,128,64]{1,2,0:T(8,128)S(1)}, s32[2]{0:T(128)}, /*index=5...) while((s32[]{:T(128)}, bf16[128,512]{0,1:T(8,128)(2,1)}, ...), condition=%wide.region_105.106_spmd.clone.clone, body=%wide.region_101.105_spmd.clone.clone.sunk | while | flops 42831240 | bytes 4827867 | solution.py:426
  655.0 24.8 %reduce-scatter.36.cloned.1.call-done = bf16[128,256]{1,0:T(8,128)(2,1)} async-done(((bf16[128,1024]{1,0:T(8,128)(2,1)}), bf16[128,256]{1,0:T(8,128)(2,1)}) %reduce-scatter.36.cloned.1.call-update) | async-done | bytes 65552 | tf_op jit(solution)/shard_map/reduce_scatter | solution.py:84
  721.8 23.4 %reduce-scatter.38.cloned.1.call-done = bf16[128,256]{1,0:T(8,128)(2,1)} async-done(((bf16[128,1024]{1,0:T(8,128)(2,1)}), bf16[128,256]{1,0:T(8,128)(2,1)}) %reduce-scatter.38.cloned.1.call-update) | async-done | bytes 65552 | tf_op jit(solution)/shard_map/reduce_scatter | solution.py:84
  782.2 26.7 %while.199 = (s32[]{:T(128)}, bf16[128,512]{0,1:T(8,128)(2,1)}, bf16[128,512]{0,1:T(8,128)(2,1)}, f32[4,128,64]{1,2,0:T(8,128)S(1)}, s32[2]{0:T(128)}, /*index=5...) while((s32[]{:T(128)}, bf16[128,512]{0,1:T(8,128)(2,1)}, ...), condition=%wide.region_122.123_spmd.clone.clone, body=%wide.region_118.122_spmd.clone.clone.sunk | while | flops 42831240 | bytes 4827867 | solution.py:426
  823.2 24.7 %reduce-scatter.40.cloned.1.call-done = bf16[128,256]{1,0:T(8,128)(2,1)} async-done(((bf16[128,1024]{1,0:T(8,128)(2,1)}), bf16[128,256]{1,0:T(8,128)(2,1)}) %reduce-scatter.40.cloned.1.call-update) | async-done | bytes 65552 | tf_op jit(solution)/shard_map/reduce_scatter | solution.py:84
  892.7 21.7 %reduce-scatter.42.cloned.1.call-done = bf16[128,256]{1,0:T(8,128)(2,1)} async-done(((bf16[128,1024]{1,0:T(8,128)(2,1)}), bf16[128,256]{1,0:T(8,128)(2,1)}) %reduce-scatter.42.cloned.1.call-update) | async-done | bytes 65552 | tf_op jit(solution)/shard_map/reduce_scatter | solution.py:84
  948.1 19.6 %while.200 = (s32[]{:T(128)}, bf16[128,512]{0,1:T(8,128)(2,1)S(1)}, bf16[128,512]{0,1:T(8,128)(2,1)S(1)}, f32[4,128,64]{1,2,0:T(8,128)S(1)}, s32[2]{0:T(128)S(1)...) while((s32[]{:T(128)}, bf16[128,512]{0,1:T(8,128)(2,1)S(1)}, ...), condition=%wide.region_139.140_spmd.clone.clone, body=%wide.region_135.139_spmd.clone.clone.sunk | while | flops 42831240 | bytes 4827867 | solution.py:426
  1024.5 10.8 reduce-scatter.48.cloned.1.call-done
  1037.0 36.1 %reduce-scatter.46.cloned.1.call-done = bf16[256,3,256]{2,0,1:T(8,128)(2,1)} async-done(((bf16[1024,3,256]{2,0,1:T(8,128)(2,1)}), bf16[256,3,256]{2,0,1:T(8,128)(2,1)}) %reduce-scatter.46.cloned.1.call-update) | async-done | bytes 393232 | tf_op jit(solution)/shard_map/reduce_scatter | solution.py:466
  1075.1 42.5 %reduce-scatter.50.cloned.1.call-done = bf16[256,1024]{1,0:T(8,128)(2,1)} async-done(((bf16[1024,1024]{1,0:T(8,128)(2,1)}), bf16[256,1024]{1,0:T(8,128)(2,1)}) %reduce-scatter.50.cloned.1.call-update) | async-done | bytes 524304 | tf_op jit(solution)/shard_map/reduce_scatter | solution.py:475
  1119.7 154.6 %all-reduce.5.cloned.1.call-done = bf16[1024,2,1024]{2,1,0:T(2,128)(2,1)} async-done(((bf16[1024,2,1024]{2,1,0:T(2,128)(2,1)}), bf16[1024,2,1024]{2,1,0:T(2,128)(2,1)}) %all-reduce.5.cloned.1.call-update) | async-done | bytes 4194320
  (1117 shorter events, 773.7 us)
Async XLA Ops:
  7.2 86.4 %reduce-scatter.22.cloned.1.call-start = ((), (), s32[]{:S(2)}) async-start(), calls=%async_computation.17 | async-start | bytes 327680 | tf_op jit(solution)/shard_map/reduce_scatter | solution.py:74
  69.1 85.6 %reduce-scatter.24.cloned.1.call-start = ((), (), s32[]{:S(2)}) async-start(), calls=%async_computation.18 | async-start | bytes 327680 | tf_op jit(solution)/shard_map/reduce_scatter | solution.py:74
  130.5 138.1 %reduce-scatter.26.cloned.1.call-start = ((), (), s32[]{:S(2)}) async-start(), calls=%async_computation.19 | async-start | bytes 327680 | tf_op jit(solution)/shard_map/reduce_scatter | solution.py:74
  246.3 83.7 %reduce-scatter.28.cloned.1.call-start = ((), (), s32[]{:S(2)}) async-start(), calls=%async_computation.20 | async-start | bytes 327680 | tf_op jit(solution)/shard_map/reduce_scatter | solution.py:74
  305.8 137.7 %reduce-scatter.30.cloned.1.call-start = ((), (), s32[]{:S(2)}) async-start(), calls=%async_computation.21 | async-start | bytes 327680 | tf_op jit(solution)/shard_map/reduce_scatter | solution.py:74
  379.7 8.2 collective-permute-start.2
  421.0 85.0 %reduce-scatter.32.cloned.1.call-start = ((), (), s32[]{:S(2)}) async-start(), calls=%async_computation.22 | async-start | bytes 327680 | tf_op jit(solution)/shard_map/reduce_scatter | solution.py:74
  481.8 95.1 %reduce-scatter.34.cloned.1.call-start = ((), (), s32[]{:S(2)}) async-start(), calls=%async_computation.23 | async-start | bytes 327680 | tf_op jit(solution)/shard_map/reduce_scatter | solution.py:84
  552.6 127.2 %reduce-scatter.36.cloned.1.call-start = ((), (), s32[]{:S(2)}) async-start(), calls=%async_computation.24 | async-start | bytes 327680 | tf_op jit(solution)/shard_map/reduce_scatter | solution.py:84
  614.0 9.5 collective-permute-start.3
  617.4 10.1 collective-permute-start.4
  655.0 90.2 %reduce-scatter.38.cloned.1.call-start = ((), (), s32[]{:S(2)}) async-start(), calls=%async_computation.25 | async-start | bytes 327680 | tf_op jit(solution)/shard_map/reduce_scatter | solution.py:84
  720.9 127.0 %reduce-scatter.40.cloned.1.call-start = ((), (), s32[]{:S(2)}) async-start(), calls=%async_computation.26 | async-start | bytes 327680 | tf_op jit(solution)/shard_map/reduce_scatter | solution.py:84
  782.2 9.6 collective-permute-start.5
  785.7 10.0 collective-permute-start.6
  823.1 91.3 %reduce-scatter.42.cloned.1.call-start = ((), (), s32[]{:S(2)}) async-start(), calls=%async_computation.27 | async-start | bytes 327680 | tf_op jit(solution)/shard_map/reduce_scatter | solution.py:84
  890.2 119.1 %reduce-scatter.52.cloned.1.call-start = ((), (), s32[]{:S(2)}) async-start(), calls=%async_computation.32 | async-start | bytes 327680
  892.7 118.3 %reduce-scatter.54.cloned.1.call-start = ((), (), s32[]{:S(2)}) async-start(), calls=%async_computation.33 | async-start | bytes 81920
  958.2 8.4 collective-permute-start.7
  971.0 51.9 %reduce-scatter.44.cloned.1.call-start = ((), (), s32[]{:S(2)}) async-start(), calls=%async_computation.28 | async-start | bytes 327680 | tf_op jit(solution)/shard_map/reduce_scatter | solution.py:84
  980.6 54.8 %reduce-scatter.48.cloned.1.call-start = ((), (), s32[]{:S(2)}) async-start(), calls=%async_computation.30 | async-start | bytes 655360 | tf_op jit(solution)/shard_map/reduce_scatter | solution.py:469
  984.1 89.0 %reduce-scatter.46.cloned.1.call-start = ((), (), s32[]{:S(2)}) async-start(), calls=%async_computation.29 | async-start | bytes 1966080 | tf_op jit(solution)/shard_map/reduce_scatter | solution.py:466
  987.8 129.8 %reduce-scatter.50.cloned.1.call-start = ((), (), s32[]{:S(2)}) async-start(), calls=%async_computation.31 | async-start | bytes 2621440 | tf_op jit(solution)/shard_map/reduce_scatter | solution.py:475
  991.9 282.4 %all-reduce.5.cloned.1.call-start = ((), (), s32[]{:S(2)}) async-start(), calls=%async_computation.34 | async-start | bytes 8388608
  (242 other events, 4753.5 us)
Sparse Core Ops, SparseCore 0:
  69.2 24.2 reduce-scatter.21
  130.6 24.0 reduce-scatter.23
  246.4 22.2 reduce-scatter.25
  305.9 24.0 reduce-scatter.27
  421.1 22.2 reduce-scatter.29
  481.9 24.0 reduce-scatter.31
  552.8 24.0 reduce-scatter.33
  655.1 24.7 reduce-scatter.35
  721.1 24.0 reduce-scatter.37
  823.3 24.6 reduce-scatter.39
  890.4 24.0 reduce-scatter.41
  916.7 16.7 reduce-scatter.51
  971.1 14.4 reduce-scatter.53
  989.1 25.0 reduce-scatter.43
  1016.8 18.5 reduce-scatter.47
  1037.5 35.5 reduce-scatter.45
  1075.9 41.6 reduce-scatter.49
  1119.9 154.3 all-reduce.4
where the time goes:
time: 1300 us; the launch traced here: 1280 us
  waiting for transfers between devices  519 us (40%)
  blocking collectives  326 us (25%)
  other arithmetic  119 us (9%)
  local copies, waits for them, and re-layouts  107 us (8%)
  matrix products  98.2 us (8%)
  starting transfers between devices  53.5 us (4%)
  loops' own time  38.8 us (3%)
  between operations  23.1 us (2%)
    psum x23, blocking collectives, row_total(): return lax.psum(jnp.sum(values, axis=1), 'tensor')  205 us
    unnamed x21, waiting for transfers between devices  155 us
    reduce_scatter x6, waiting for transfers between devices, to_cols(): lax.psum_scatter(partial_sum.astype(jnp.bfloat16), 'tensor', scatter_dime...  134 us
    reduce_scatter x6, waiting for transfers between devices, grad_cols(): lax.psum_scatter(partial_sum.astype(jnp.bfloat16), 'tensor', scatter_dime...  117 us
    all_gather x6, blocking collectives, full_rows(): return lax.all_gather(columns, 'tensor', axis=1, tiled=True)  55.7 us
    all_gather x6, blocking collectives, grad_rows(): return lax.all_gather(columns, 'tensor', axis=1, tiled=True)  55.5 us
    reduce_scatter x1, waiting for transfers between devices, per_device(): lax.psum_scatter(grad_totals[3].astype(jnp.bfloat16), 'dp', scatter_dimen...  42.5 us
    ppermute x16, starting transfers between devices, from_behind(): return lax.ppermute(array, axis, pairs)  39.8 us
  transfers between devices with their start and end apart: 43, of which 30 were waited for; matrix products, arithmetic and copies ran while one was open for 8% of the time, Pallas kernels for 0%

commit v1 on v0

--- a/solution.py
+++ b/solution.py
@@ -1,8 +1,12 @@
+import functools
 import math
+import types
 
 import jax
 import jax.numpy as jnp
 from jax import lax
+from jax.experimental import pallas as pl
+from jax.experimental.pallas import tpu as pltpu
 from jax.sharding import PartitionSpec as P
 
 D = 1024
@@ -27,7 +31,9 @@
 
 
 def seq_table(lengths_row, positions):
-    seq_end = jnp.cumsum(lengths_row)
+    count = lengths_row.shape[0]
+    order = jnp.arange(count, dtype=jnp.int32)
+    seq_end = jnp.sum(jnp.where(order[None, :] <= order[:, None], lengths_row[None, :], 0), axis=1)
     seq_start = seq_end - lengths_row
     segment = jnp.sum((positions[:, None] >= seq_end[None, :]).astype(jnp.int32), axis=1)
     labels = jnp.arange(lengths_row.shape[0], dtype=jnp.int32)
@@ -498,6 +504,698 @@
     )
 
 
+MESH = pl.DeviceIdType.MESH
+MICRO = 2
+F32 = jnp.float32
+BF16 = jnp.bfloat16
+
+
+def mul(left_op, right_op):
+    return jnp.dot(left_op, right_op, preferred_element_type=F32)
+
+
+def remote(src, dst, send_sem, recv_sem, device):
+    return pltpu.make_async_remote_copy(
+        src_ref=src, dst_ref=dst, send_sem=send_sem, recv_sem=recv_sem, device_id=device, device_id_type=MESH
+    )
+
+
+def ball(values, width):
+    ratio = lax.rsqrt(jnp.sum(values * values, axis=1, keepdims=True) / width + EPSILON)
+    return values * ratio, ratio
+
+
+def ball_back(source, ratio, grad_in, width):
+    inner = jnp.sum(grad_in * source, axis=1, keepdims=True)
+    return ratio * grad_in - source * (ratio * ratio * ratio) * (inner / width)
+
+
+def buffers(nt, nz, rows, width, cols, hidden, shard, section, chunk):
+    vmem, dma = pltpu.VMEM, pltpu.SemaphoreType.DMA
+    pair = 2 * rows
+    return dict(
+        wq=vmem((2, 3, width, cols), BF16),
+        wo=vmem((2, cols, width), BF16),
+        wu=vmem((2, 2, width, hidden), BF16),
+        wd=vmem((2, hidden, width), BF16),
+        par=vmem((2, 8, hidden), F32),
+        alp=vmem((2, 8, width), F32),
+        full_in=vmem((2, rows, width), BF16),
+        mid_full=vmem((2, rows, width), BF16),
+        dml_full=vmem((2, rows, width), BF16),
+        dat_full=vmem((2, rows, width), BF16),
+        fi_p=vmem((rows, width), BF16),
+        at_p=vmem((rows, cols), BF16),
+        da_p=vmem((rows, width), BF16),
+        dq_p=vmem((rows, 3 * cols), BF16),
+        xa=vmem((nt, nz * 2 * shard, width), BF16),
+        da=vmem((nt, nz * 2 * shard, width), BF16),
+        kv=vmem((2, pair, 2 * cols), BF16),
+        dkv_f=vmem((pair, 2 * cols), F32),
+        dkv_s=vmem((2, rows, 2 * cols), BF16),
+        dkv_r=vmem((2, rows, 2 * cols), BF16),
+        rs_s=vmem((8, rows, width), BF16),
+        rs_r=vmem((8, nt - 1, shard, width), BF16),
+        rot=vmem((2, 2, rows, cols), F32),
+        rat=vmem((2, 2, rows, cols), F32),
+        qb=vmem((2, rows, cols), BF16),
+        prob=vmem((2, cols // HEAD_DIM, rows, pair), F32),
+        at=vmem((2, rows, cols), BF16),
+        araw=vmem((2, shard, width), F32),
+        mraw=vmem((2, shard, width), F32),
+        mid=vmem((2, shard, width), F32),
+        zone=vmem((2, shard, width), F32),
+        ztwo=vmem((2, shard, width), F32),
+        up=vmem((2, rows, hidden), F32),
+        gate=vmem((2, rows, hidden), F32),
+        act=vmem((rows, hidden), BF16),
+        duv=vmem((2, rows, hidden), BF16),
+        dqkv=vmem((2, rows, 3 * cols), BF16),
+        cot_rows=vmem((shard, width), BF16),
+        out_s=vmem((2, shard, width), BF16),
+        ig_s=vmem((2, shard, width), BF16),
+        cosb=vmem((rows, cols), F32),
+        sinb=vmem((rows, cols), F32),
+        bias=vmem((rows, pair), F32),
+        blk=vmem((cols, cols), BF16),
+        al_s=vmem((2, 8, width), F32),
+        al_r=vmem((2, nt - 1, 8, cols), F32),
+        small=vmem((2, 8, cols), F32),
+        sm_r=vmem((nz, 2, 8, cols), F32),
+        wq_s=vmem((nz - 1, section, 3 * cols), BF16),
+        wq_r=vmem((nz - 1, section, 3 * cols), BF16),
+        wo_f=vmem((cols, width), F32),
+        wo_s=vmem((cols, width), BF16),
+        wo_r=vmem((nz - 1, chunk, width), BF16),
+        act_b=vmem((nz * 2 * shard, hidden), BF16),
+        suv_b=vmem((2, hidden), F32),
+        acc=vmem((2, section, hidden), F32),
+        w_l=dma((2, 4)), w_rs=dma((4,)),
+        par_l=dma((2,)), par_s=dma((1,)),
+        alp_r=dma((2, nt)), alp_s=dma((2, nt)),
+        hid_r=dma((nt,)), hid_s=dma((2, nt)),
+        cot_r=dma((nt,)), cot_s=dma((2, nt)),
+        fi_rs=dma((2,)), at_rs=dma((2,)), dap_rs=dma((2,)), dq_rs=dma((2,)),
+        kv_rs=dma((2, 2)), dkv_rs=dma((2, 2)),
+        ag_ss=dma((7, nt - 1)), ag_rr=dma((7, nt - 1)),
+        rs_ss=dma((8, nt - 1)), rs_rr=dma((8, nt - 1)),
+        xa_r=dma((nz, 2)), xa_ss=dma((2, nz)),
+        da_r=dma((nz, 2)), da_ss=dma((2, nz)),
+        xf_ss=dma((nt - 1,)), xf_rr=dma((nt - 1,)), df_ss=dma((nt - 1,)), df_rr=dma((nt - 1,)),
+        lo_ss=dma((2, nt)), lo_r=dma((2, nt)),
+        ig_ss=dma((2, nt)), ig_r=dma((2, nt)),
+        al_ss=dma((2, nt - 1)), al_rr=dma((2, nt - 1)),
+        sm_ss=dma((2, nz)), sm_rr=dma((nz, 2)),
+        wq_ss=dma((nz - 1,)), wq_rr=dma((nz - 1,)),
+        wo_ss=dma((nz - 1,)), wo_rr=dma((nz - 1,)),
+    )
+
+
+def fused_kernel(names, nt, nz, *refs):
+    hid, cot, lens, wq_in, wo_in, wu_in, wd_in, par_in, rates = refs[:9]
+    lo, ig, gq, go, gu, gd, gsqk, gsuv, gal = refs[9:18]
+    b = types.SimpleNamespace(**dict(zip(names, refs[18:])))
+    rows, width = b.full_in.shape[1:]
+    cols, hidden = b.qb.shape[2], b.wd.shape[1]
+    shard = b.mid.shape[1]
+    heads = cols // HEAD_DIM
+    pair = 2 * rows
+    section_rows = width // nz
+    chunk = cols // nz
+    tile = 512
+    s, t, z = lax.axis_index("section"), lax.axis_index("tensor"), lax.axis_index("dp")
+    p = lax.rem(z, 2)
+    base = z - p
+    peer = (1 - s, t, z)
+    pending = []
+
+    def around(k):
+        return lax.rem(t + k, nt)
+
+    def along(k):
+        return lax.rem(z + k, nz)
+
+    def later(copy, when=None):
+        pending.append((copy, when))
+
+    def lanes(index, size):
+        return pl.ds(pl.multiple_of(index * size, size), size)
+
+    weights = [(wq_in, b.wq), (wo_in, b.wo), (wu_in, b.wu), (wd_in, b.wd)]
+    for i, (src, dst) in enumerate(weights):
+        pltpu.make_async_copy(src, dst.at[s], b.w_l.at[s, i]).start()
+    pltpu.make_async_copy(par_in.at[:, pl.ds(0, hidden)], b.par.at[s], b.par_l.at[s]).start()
+
+    barrier = pltpu.get_barrier_semaphore()
+    greeted = 0
+    for dz in range(2):
+        for dt in range(nt):
+            for dc in range(2):
+                if dz or dt or dc:
+                    device = (lax.rem(s + dc, 2), around(dt), base + lax.rem(p + dz, 2))
+                    pl.semaphore_signal(barrier, inc=1, device_id=device, device_id_type=MESH)
+                    greeted += 1
+    for dz in range(2, nz):
+        for dc in range(2):
+            device = (lax.rem(s + dc, 2), t, lax.rem(base + dz, nz))
+            pl.semaphore_signal(barrier, inc=1, device_id=device, device_id_type=MESH)
+            greeted += 1
+    pl.semaphore_wait(barrier, greeted)
+
+    is_source = s == p
+    for src, rs, ss in ((hid, b.hid_r, b.hid_s), (cot, b.cot_r, b.cot_s)):
+        for dz in range(2):
+            to_mb = lax.rem(p + dz, 2)
+            for dt in range(nt):
+                to_t = around(dt)
+                if src is hid:
+                    piece, place = src.at[to_mb], b.full_in.at[0, :, lanes(t, cols)]
+                else:
+                    piece = src.at[to_mb, pl.ds(pl.multiple_of(to_t * shard, shard), shard), :]
+                    place = b.cot_rows.at[:, lanes(t, cols)]
+                if dz == 0 and dt == 0:
+
+                    @pl.when(is_source)
+                    def _(piece=piece, place=place, rs=rs):
+                        pltpu.make_async_copy(piece, place, rs.at[0]).start()
+                else:
+                    copy = remote(piece, place, ss.at[dz, dt], rs.at[dt], (s, to_t, base + to_mb))
+                    pl.when(is_source)(copy.start)
+                    later(copy, is_source)
+        if src is hid:
+            copy = remote(par_in.at[:, pl.ds(0, hidden)], b.par.at[s], b.par_s.at[0], b.par_l.at[s], peer)
+            copy.start()
+            later(copy)
+            alp_src, alp_dst = par_in.at[:, pl.ds(hidden, cols)], b.alp.at[s, :, lanes(t, cols)]
+            for dc in range(2):
+                for dt in range(nt):
+                    if dc == 0 and dt == 0:
+                        pltpu.make_async_copy(alp_src, alp_dst, b.alp_r.at[s, 0]).start()
+                    else:
+                        copy = remote(alp_src, alp_dst, b.alp_s.at[dc, dt], b.alp_r.at[s, dt], (lax.rem(s + dc, 2), around(dt), z))
+                        copy.start()
+                        later(copy)
+            for i, (src_w, dst_w) in enumerate(weights):
+                copy = remote(src_w, dst_w.at[s], b.w_rs.at[i], b.w_l.at[s, i], peer)
+                copy.start()
+                later(copy)
+
+    def wait_weight(layer, i):
+        src_w, dst_w = weights[i]
+        pltpu.make_async_copy(src_w, dst_w.at[layer], b.w_l.at[layer, i]).wait()
+
+    token0 = (base // 2) * pair
+    pos_q = token0 + s * rows + lax.broadcasted_iota(jnp.int32, (rows, 1), 0)
+    pos_k = token0 + lax.broadcasted_iota(jnp.int32, (1, pair), 1)
+
+    def sequences(pos):
+        seg = jnp.zeros_like(pos)
+        first = jnp.zeros_like(pos)
+        end = jnp.int32(0)
+        for i in range(lens.shape[1]):
+            end = end + lens[p, i]
+            past = pos >= end
+            seg = seg + past.astype(jnp.int32)
+            first = jnp.where(past, end, first)
+        return seg, pos - first
+
+    seg_q, place_q = sequences(pos_q)
+    seg_k, _ = sequences(pos_k)
+    allowed = (seg_q == seg_k) & (pos_k <= pos_q)
+    b.bias[...] = jnp.where(allowed, 0.0, NEG_LARGE)
+    angle = place_q.astype(F32) * rates[...]
+    b.cosb[...] = jnp.cos(angle)
+    b.sinb[...] = jnp.sin(angle)
+    col = lax.broadcasted_iota(jnp.int32, (1, cols), 1)
+    lower = (col & (HEAD_DIM // 2)) == 0
+    head_of = lax.shift_right_logical(col, 6)
+    head_row = lax.shift_right_logical(lax.broadcasted_iota(jnp.int32, (cols, 1), 0), 6)
+    b.blk[...] = jnp.where(head_row == head_of, 1.0, 0.0).astype(BF16)
+    picks = [jnp.where(head_of == h, 1.0, 0.0) for h in range(heads)]
+    b.al_s[...] = jnp.zeros_like(b.al_s)
+    b.small[...] = jnp.zeros_like(b.small)
+
+    def partner_cols(x):
+        half = HEAD_DIM // 2
+        return jnp.where(lower, -pltpu.roll(x, cols - half, 1), pltpu.roll(x, half, 1))
+
+    def head_total(x):
+        high = x.astype(BF16)
+        low = (x - high.astype(F32)).astype(BF16)
+        return mul(high, b.blk[...]) + mul(low, b.blk[...])
+
+    def gather(stage, ref):
+        mine = ref.at[pl.ds(pl.multiple_of(t * shard, shard), shard), :]
+        for k in range(1, nt):
+            copy = remote(mine, mine, b.ag_ss.at[stage, k - 1], b.ag_rr.at[stage, k - 1], (s, around(k), z))
+            copy.start()
+            later(copy)
+
+    def gather_wait(stage, ref):
+        for k in range(1, nt):
+            theirs = ref.at[pl.ds(pl.multiple_of(around(nt - k) * shard, shard), shard), :]
+            remote(theirs, theirs, b.ag_ss.at[stage, k - 1], b.ag_rr.at[stage, k - 1], (s, around(k), z)).wait_recv()
+
+    def scatter(stage):
+        for k in range(1, nt):
+            piece = b.rs_s.at[stage, pl.ds(pl.multiple_of(around(k) * shard, shard), shard), :]
+            copy = remote(piece, b.rs_r.at[stage, k - 1], b.rs_ss.at[stage, k - 1], b.rs_rr.at[stage, k - 1], (s, around(k), z))
+            copy.start()
+            later(copy)
+
+    def scatter_wait(stage):
+        total = b.rs_s[stage, pl.ds(pl.multiple_of(t * shard, shard), shard), :].astype(F32)
+        for k in range(1, nt):
+            place = b.rs_r.at[stage, k - 1]
+            remote(place, place, b.rs_ss.at[stage, k - 1], b.rs_rr.at[stage, k - 1], (s, around(k), z)).wait_recv()
+            total = total + place[...].astype(F32)
+        return total
+
+    slot = pl.ds(pl.multiple_of((z * 2 + s) * shard, shard), shard)
+
+    def my_rows(ref):
+        return ref.at[pl.ds(pl.multiple_of(t * shard, shard), shard), :]
+
+    def to_owner(layer, ref, place_of, send_sems, recv_sems):
+        for k in range(nz):
+            copy = remote(ref, place_of, send_sems.at[layer, k], recv_sems.at[k, s], (layer, t, along(k)))
+            if k == 0:
+
+                @pl.when(s == layer)
+                def _():
+                    pltpu.make_async_copy(ref, place_of, recv_sems.at[0, s]).start()
+
+                pl.when(s != layer)(copy.start)
+                later(copy, s != layer)
+            else:
+                copy.start()
+                later(copy)
+
+    def bundle(layer, ref, recv_sems, fwd_ss, fwd_rr):
+        @pl.when(s == layer)
+        def _():
+            for k in range(nz):
+                for core in range(2):
+                    row = pl.multiple_of((along(nz - k) * 2 + core) * shard, shard)
+                    place = ref.at[t, pl.ds(row, shard), :]
+                    pltpu.make_async_copy(place, place, recv_sems.at[k, core]).wait()
+
+        for k in range(1, nt):
+            copy = remote(ref.at[t], ref.at[t], fwd_ss.at[k - 1], fwd_rr.at[k - 1], (s, around(k), z))
+            pl.when(s == layer)(copy.start)
+            later(copy, s == layer)
+
+    def to_output(layer, ref, out, send_sems, recv_sems):
+        to_z = base + s
+        place = out.at[p, pl.ds(pl.multiple_of(t * shard, shard), shard), :]
+        for k in range(nt):
+            to_t = around(k)
+            piece = ref.at[:, lanes(to_t, cols)]
+            copy = remote(piece, place, send_sems.at[layer, k], recv_sems.at[p, k], (layer, to_t, to_z))
+            if k == 0:
+                here = (s == layer) & (to_z == z)
+
+                @pl.when(here)
+                def _(piece=piece):
+                    pltpu.make_async_copy(piece, place, recv_sems.at[p, 0]).start()
+
+                away = jnp.logical_not(here)
+                pl.when(away)(copy.start)
+                later(copy, away)
+            else:
+                copy.start()
+                later(copy)
+
+    for layer in range(2):
+        full_in = b.full_in.at[layer]
+        if layer == 0:
+            for dt in range(nt):
+                place = b.full_in.at[0, :, lanes(around(nt - dt), cols)]
+                pltpu.make_async_copy(hid.at[0], place, b.hid_r.at[dt]).wait()
+            for src_core in range(2):
+                pltpu.make_async_copy(par_in.at[:, pl.ds(0, hidden)], b.par.at[src_core], b.par_l.at[src_core]).wait()
+                for dt in range(nt):
+                    place = b.alp.at[src_core, :, lanes(around(nt - dt), cols)]
+                    pltpu.make_async_copy(par_in.at[:, pl.ds(hidden, cols)], place, b.alp_r.at[src_core, dt]).wait()
+        else:
+            gather_wait(6, full_in)
+            bundle(0, b.xa, b.xa_r, b.xf_ss, b.xf_rr)
+        copy = remote(full_in, b.fi_p, b.fi_rs.at[0], b.fi_rs.at[1], peer)
+        pl.when(s != layer)(copy.start)
+        later(copy, s != layer)
+        scale_qk = b.par[layer, 2:3, 0:cols]
+        wait_weight(layer, 0)
+        x = full_in[...]
+        own = pl.ds(pl.multiple_of(s * rows, rows), rows)
+        for i in range(2):
+            raw = mul(x, b.wq[layer, i])
+            rotated = raw * b.cosb[...] + partner_cols(raw) * b.sinb[...]
+            ratio = lax.rsqrt(head_total(rotated * rotated) / HEAD_DIM + EPSILON)
+            b.rot[layer, i] = rotated
+            b.rat[layer, i] = ratio
+            normed = (rotated * ratio * scale_qk).astype(BF16)
+            if i == 0:
+                b.qb[layer] = normed
+            else:
+                b.kv[layer, own, 0:cols] = normed
+        b.kv[layer, own, cols : 2 * cols] = mul(x, b.wq[layer, 2]).astype(BF16)
+        mine = b.kv.at[layer, own, :]
+        copy = remote(mine, mine, b.kv_rs.at[layer, 0], b.kv_rs.at[layer, 1], peer)
+        copy.start()
+        later(copy)
+        copy.wait_recv()
+        att = jnp.zeros((rows, cols), F32)
+        for h in range(heads):
+            q_h = (b.qb[layer].astype(F32) * picks[h]).astype(BF16)
+            scores = contract_cols(q_h, b.kv[layer, :, 0:cols]) * (1.0 / math.sqrt(HEAD_DIM)) + b.bias[...]
+            top = jnp.max(scores, axis=1, keepdims=True)
+            terms = jnp.exp(scores - top)
+            prob = terms / jnp.sum(terms, axis=1, keepdims=True)
+            b.prob[layer, h] = prob
+            att = att + picks[h] * mul(prob.astype(BF16), b.kv[layer, :, cols : 2 * cols])
+        b.at[layer] = att.astype(BF16)
+        wait_weight(layer, 1)
+        for n in range(0, width, tile):
+            b.rs_s[layer, :, n : n + tile] = mul(b.at[layer], b.wo[layer, :, n : n + tile]).astype(BF16)
+        scatter(layer)
+        hin = my_rows(full_in)[...].astype(F32)
+        rate_a = b.alp[layer, 0:1, :]
+        rate_m = b.alp[layer, 1:2, :]
+        araw = scatter_wait(layer)
+        b.araw[layer] = araw
+        zone = hin + rate_a * (ball(araw, width)[0] - hin)
+        b.zone[layer] = zone
+        mid = ball(zone, width)[0]
+        b.mid[layer] = mid
+        mid_full = b.mid_full.at[layer]
+        my_rows(mid_full)[...] = mid.astype(BF16)
+        gather(layer, mid_full)
+        to_owner(layer, my_rows(mid_full), b.xa.at[t, slot, :], b.xa_ss, b.xa_r)
+        wait_weight(layer, 2)
+        wait_weight(layer, 3)
+        gather_wait(layer, mid_full)
+        x = mid_full[...]
+        for n in range(0, hidden, tile):
+            cut = slice(n, n + tile)
+            up = mul(x, b.wu[layer, 0, :, cut])
+            gate = mul(x, b.wu[layer, 1, :, cut])
+            b.up[layer, :, cut] = up
+            b.gate[layer, :, cut] = gate
+            gate_s = gate * b.par[layer, 1:2, cut]
+            b.act[:, cut] = (up * b.par[layer, 0:1, cut] * (gate_s / (1.0 + jnp.exp(-gate_s)))).astype(BF16)
+        for n in range(0, width, tile):
+            b.rs_s[2 + layer, :, n : n + tile] = mul(b.act[...], b.wd[layer, :, n : n + tile]).astype(BF16)
+        scatter(2 + layer)
+        mraw = scatter_wait(2 + layer)
+        b.mraw[layer] = mraw
+        ztwo = mid + rate_m * (ball(mraw, width)[0] - mid)
+        b.ztwo[layer] = ztwo
+        b.out_s[layer] = ball(ztwo, width)[0].astype(BF16)
+        if layer == 0:
+            my_rows(b.full_in.at[1])[...] = b.out_s[0]
+            gather(6, b.full_in.at[1])
+        to_output(layer, b.out_s.at[layer], lo, b.lo_ss, b.lo_r)
+
+    for dt in range(nt):
+        place = b.cot_rows.at[:, lanes(around(nt - dt), cols)]
+        pltpu.make_async_copy(cot.at[0, pl.ds(0, shard), :], place, b.cot_r.at[dt]).wait()
+    grad_out = b.cot_rows[...].astype(F32)
+    for layer in (1, 0):
+        own = pl.ds(pl.multiple_of(s * rows, rows), rows)
+        other = pl.ds(pl.multiple_of((1 - s) * rows, rows), rows)
+        rate_a = b.alp[layer, 0:1, :]
+        rate_m = b.alp[layer, 1:2, :]
+        scale_qk = b.par[layer, 2:3, 0:cols]
+        mid = b.mid[layer]
+        mraw_n, ratio_m = ball(b.mraw[layer], width)
+        ratio_two = ball(b.ztwo[layer], width)[1]
+        d_two = ball_back(b.ztwo[layer], ratio_two, grad_out, width)
+        d_mid = (1.0 - rate_m) * d_two
+        b.al_s[layer, 1:2, :] = jnp.sum(d_two * (mraw_n - mid), axis=0, keepdims=True)
+        dml_full = b.dml_full.at[layer]
+        my_rows(dml_full)[...] = ball_back(b.mraw[layer], ratio_m, rate_m * d_two, width).astype(BF16)
+        gather(2 + layer, dml_full)
+        to_owner(layer, my_rows(dml_full), b.da.at[t, slot, :], b.da_ss, b.da_r)
+        gather_wait(2 + layer, dml_full)
+        if layer == 1:
+            bundle(1, b.xa, b.xa_r, b.xf_ss, b.xf_rr)
+        x = dml_full[...]
+        for n in range(0, hidden, tile):
+            cut = slice(n, n + tile)
+            d_act = contract_cols(x, b.wd[layer, cut, :])
+            scale_up, scale_gate = b.par[layer, 0:1, cut], b.par[layer, 1:2, cut]
+            up_s = b.up[layer, :, cut] * scale_up
+            gate_s = b.gate[layer, :, cut] * scale_gate
+            sig = 1.0 / (1.0 + jnp.exp(-gate_s))
+            b.duv[0, :, cut] = (d_act * gate_s * sig * scale_up).astype(BF16)
+            b.duv[1, :, cut] = (d_act * up_s * sig * (1.0 + gate_s * (1.0 - sig)) * scale_gate).astype(BF16)
+        for n in range(0, width, tile):
+            cut = slice(n, n + tile)
+            part = contract_cols(b.duv[0], b.wu[layer, 0, cut, :]) + contract_cols(b.duv[1], b.wu[layer, 1, cut, :])
+            b.rs_s[4 + layer, :, cut] = part.astype(BF16)
+        scatter(4 + layer)
+        hin = my_rows(b.full_in.at[layer])[...].astype(F32)
+        araw_n, ratio_a = ball(b.araw[layer], width)
+        ratio_one = ball(b.zone[layer], width)[1]
+        d_mid = d_mid + scatter_wait(4 + layer)
+        d_one = ball_back(b.zone[layer], ratio_one, d_mid, width)
+        b.al_s[layer, 0:1, :] = jnp.sum(d_one * (araw_n - hin), axis=0, keepdims=True)
+        dat_full = b.dat_full.at[layer]
+        my_rows(dat_full)[...] = ball_back(b.araw[layer], ratio_a, rate_a * d_one, width).astype(BF16)
+        gather(4 + layer, dat_full)
+        for k in range(1, nt):
+            copy = remote(b.al_s.at[layer, :, lanes(around(k), cols)], b.al_r.at[layer, k - 1], b.al_ss.at[layer, k - 1], b.al_rr.at[layer, k - 1], (s, around(k), z))
+            copy.start()
+            later(copy)
+        gather_wait(4 + layer, dat_full)
+        bundle(layer, b.da, b.da_r, b.df_ss, b.df_rr)
+        for src_v, dst_v, sems in ((dat_full, b.da_p, b.dap_rs), (b.at.at[layer], b.at_p, b.at_rs)):
+            copy = remote(src_v, dst_v, sems.at[0], sems.at[1], peer)
+            pl.when(s != layer)(copy.start)
+            later(copy, s != layer)
+        d_att = contract_cols(dat_full[...], b.wo[layer])
+        dq = jnp.zeros((rows, cols), F32)
+        dk = jnp.zeros((pair, cols), F32)
+        dv = jnp.zeros((pair, cols), F32)
+        for h in range(heads):
+            d_att_h = (d_att * picks[h]).astype(BF16)
+            q_h = (b.qb[layer].astype(F32) * picks[h]).astype(BF16)
+            prob = b.prob[layer, h]
+            d_prob = contract_cols(d_att_h, b.kv[layer, :, cols : 2 * cols])
+            d_score = (prob * (d_prob - jnp.sum(prob * d_prob, axis=1, keepdims=True))).astype(BF16)
+            dv = dv + contract_rows(prob.astype(BF16), d_att_h)
+            dq = dq + picks[h] * mul(d_score, b.kv[layer, :, 0:cols])
+            dk = dk + contract_rows(d_score, q_h)
+        b.dkv_f[:, 0:cols] = dk * (1.0 / math.sqrt(HEAD_DIM))
+        b.dkv_f[:, cols : 2 * cols] = dv
+        b.dkv_s[layer] = b.dkv_f[other, :].astype(BF16)
+        copy = remote(b.dkv_s.at[layer], b.dkv_r.at[layer], b.dkv_rs.at[layer, 0], b.dkv_rs.at[layer, 1], peer)
+        copy.start()
+        later(copy)
+        d_scale = jnp.zeros((1, cols), F32)
+        for i in range(2):
+            if i == 0:
+                grad_n = dq * (1.0 / math.sqrt(HEAD_DIM))
+            else:
+                copy.wait_recv()
+                grad_n = b.dkv_f[own, 0:cols] + b.dkv_r[layer, :, 0:cols].astype(F32)
+            rotated, ratio = b.rot[layer, i], b.rat[layer, i]
+            d_scale = d_scale + jnp.sum(grad_n * rotated * ratio, axis=0, keepdims=True)
+            d_unit = grad_n * scale_qk
+            d_rot = ratio * d_unit - rotated * (ratio * ratio * ratio) * (head_total(d_unit * rotated) / HEAD_DIM)
+            d_raw = d_rot * b.cosb[...] - partner_cols(d_rot * b.sinb[...])
+            b.dqkv[layer, :, i * cols : (i + 1) * cols] = d_raw.astype(BF16)
+        d_val = b.dkv_f[own, cols : 2 * cols] + b.dkv_r[layer, :, cols : 2 * cols].astype(F32)
+        b.dqkv[layer, :, 2 * cols : 3 * cols] = d_val.astype(BF16)
+        for n in range(0, width, tile):
+            part = contract_cols(b.dqkv[layer, :, 0:cols], b.wq[layer, 0, n : n + tile, :])
+            for i in range(1, 3):
+                part = part + contract_cols(b.dqkv[layer, :, i * cols : (i + 1) * cols], b.wq[layer, i, n : n + tile, :])
+            b.rs_s[6 + layer, :, n : n + tile] = part.astype(BF16)
+        scatter(6 + layer)
+        copy = remote(b.dqkv.at[layer], b.dq_p, b.dq_rs.at[0], b.dq_rs.at[1], peer)
+        pl.when(s != layer)(copy.start)
+        later(copy, s != layer)
+        total = b.al_s[layer, :, lanes(t, cols)]
+        for k in range(1, nt):
+            place = b.al_r.at[layer, k - 1]
+            remote(place, place, b.al_ss.at[layer, k - 1], b.al_rr.at[layer, k - 1], peer).wait_recv()
+            total = total + place[...]
+        b.small[layer] = total
+        b.small[layer, 2:3, :] = d_scale
+        to_owner(layer, b.small.at[layer], b.sm_r.at[lax.rem(z, nz), s], b.sm_ss, b.sm_rr)
+
+        @pl.when(s == layer)
+        def _(layer=layer):
+            for dst_v, sems in ((b.fi_p, b.fi_rs), (b.da_p, b.dap_rs), (b.at_p, b.at_rs), (b.dq_p, b.dq_rs)):
+                remote(dst_v, dst_v, sems.at[0], sems.at[1], peer).wait_recv()
+            for k in (1, 2, 3, 0):
+                cut = lanes(along(k), section_rows)
+                part = contract_rows(b.full_in[layer, :, cut], b.dqkv[layer]) + contract_rows(b.fi_p[:, cut], b.dq_p[...])
+                if k:
+                    b.wq_s[k - 1] = part.astype(BF16)
+                    remote(b.wq_s.at[k - 1], b.wq_r.at[k - 1], b.wq_ss.at[k - 1], b.wq_rr.at[k - 1], (layer, t, along(k))).start()
+                else:
+                    for i in range(3):
+                        gq[i] = part[:, i * cols : (i + 1) * cols]
+            for n in range(0, width, tile):
+                cut = slice(n, n + tile)
+                part = contract_rows(b.at[layer], b.dat_full[layer, :, cut]) + contract_rows(b.at_p[...], b.da_p[:, cut])
+                b.wo_f[:, cut] = part
+                b.wo_s[:, cut] = part.astype(BF16)
+            for k in range(1, nz):
+                piece = b.wo_s.at[pl.ds(pl.multiple_of(along(k) * chunk, chunk), chunk), :]
+                remote(piece, b.wo_r.at[k - 1], b.wo_ss.at[k - 1], b.wo_rr.at[k - 1], (layer, t, along(k))).start()
+
+        d_hin = (1.0 - rate_a) * d_one + scatter_wait(6 + layer)
+        b.ig_s[layer] = d_hin.astype(BF16)
+        to_output(layer, b.ig_s.at[layer], ig, b.ig_ss, b.ig_r)
+        grad_out = b.ig_s[layer].astype(F32)
+
+    mine_cols = lanes(z, section_rows)
+    for ref in (b.acc, gd, gsuv):
+        ref[...] = jnp.zeros_like(ref)
+    suv_total = jnp.zeros((2, hidden), F32)
+
+    def block(k, suv_now):
+        at = lax.rem(t + nt - k, nt)
+
+        @pl.when(k > 0)
+        def _():
+            for ref, ss, rr in ((b.xa, b.xf_ss, b.xf_rr), (b.da, b.df_ss, b.df_rr)):
+                remote(ref.at[at], ref.at[at], ss.at[k - 1], rr.at[k - 1], peer).wait_recv()
+
+        new = []
+        for n in range(0, hidden, tile):
+            cut = slice(n, n + tile)
+            up = mul(b.xa[at], b.wu[s, 0, :, cut])
+            gate = mul(b.xa[at], b.wu[s, 1, :, cut])
+            d_act = contract_cols(b.da[at], b.wd[s, cut, :])
+            scale_up, scale_gate = b.par[s, 0:1, cut], b.par[s, 1:2, cut]
+            up_s = up * scale_up
+            gate_s = gate * scale_gate
+            sig = 1.0 / (1.0 + jnp.exp(-gate_s))
+            b.act_b[:, cut] = (up_s * gate_s * sig).astype(BF16)
+            d_up = d_act * gate_s * sig
+            d_gate = d_act * up_s * sig * (1.0 + gate_s * (1.0 - sig))
+            new.append((jnp.sum(d_up * up, axis=0, keepdims=True), jnp.sum(d_gate * gate, axis=0, keepdims=True)))
+            x_cut = b.xa[at, :, mine_cols]
+            b.acc[0, :, cut] += contract_rows(x_cut, (d_up * scale_up).astype(BF16))
+            b.acc[1, :, cut] += contract_rows(x_cut, (d_gate * scale_gate).astype(BF16))
+        for n in range(0, width, tile):
+            gd[:, n : n + tile] += contract_rows(b.act_b[:, lanes(z, hidden // nz)], b.da[at, :, n : n + tile])
+        return tuple(
+            jnp.concatenate([pair_of[i] for pair_of in new], axis=1) + suv_now[i] for i in range(2)
+        )
+
+    suv = lax.fori_loop(0, nt, block, (suv_total[0:1], suv_total[1:2]))
+    for i in range(2):
+        b.suv_b[i : i + 1, :] = suv[i]
+    gsuv[...] = b.suv_b[:, lanes(z, hidden // nz)]
+    per_row = 2 * hidden // 128
+    for j in range(hidden // 128):
+        for i in range(2):
+            gu[pl.ds(2 * j + i, section_rows, stride=per_row), :] = b.acc[i, :, j * 128 : (j + 1) * 128]
+
+    for k in range(1, nz):
+        place = b.wq_r.at[k - 1]
+        remote(place, place, b.wq_ss.at[k - 1], b.wq_rr.at[k - 1], peer).wait_recv()
+        for i in range(3):
+            gq[i] += b.wq_r[k - 1, :, i * cols : (i + 1) * cols].astype(F32)
+    total = b.wo_f[pl.ds(pl.multiple_of(z * chunk, chunk), chunk), :]
+    for k in range(1, nz):
+        place = b.wo_r.at[k - 1]
+        remote(place, place, b.wo_ss.at[k - 1], b.wo_rr.at[k - 1], peer).wait_recv()
+        total = total + place[...].astype(F32)
+    go[...] = total
+    total = jnp.zeros((8, cols), F32)
+    for k in range(nz):
+        for core in range(2):
+            place = b.sm_r.at[lax.rem(z + nz - k, nz), core]
+            pltpu.make_async_copy(place, place, b.sm_rr.at[k, core]).wait()
+            total = total + place[...]
+    turned = pltpu.roll(total, lax.rem(cols - z * chunk, cols), 1)
+    gal[...] = turned[0:2, 0:chunk]
+    gsqk[...] = turned[2:3, 0:chunk]
+    for out, sems in ((lo, b.lo_r), (ig, b.ig_r)):
+        for m in range(2):
+            for k in range(nt):
+                place = out.at[m, pl.ds(pl.multiple_of(around(nt - k) * shard, shard), shard), :]
+                pltpu.make_async_copy(place, place, sems.at[m, k]).wait()
+    for k in range(nz - 1):
+        remote(b.wq_s.at[k], b.wq_r.at[k], b.wq_ss.at[k], b.wq_rr.at[k], peer).wait_send()
+        piece = b.wo_s.at[pl.ds(0, chunk), :]
+        remote(piece, b.wo_r.at[k], b.wo_ss.at[k], b.wo_rr.at[k], peer).wait_send()
+    for copy, when in pending:
+        if when is None:
+            copy.wait_send()
+        else:
+            pl.when(when)(copy.wait_send)
+
+
+def per_device_fused(hidden_in, cotangent, lengths, w_qkv, w_out, w_ug, w_down, s_qk, s_uv, alpha):
+    nt, nz = lax.axis_size("tensor"), lax.axis_size("dp")
+    rows, cols = hidden_in.shape[1:]
+    width, hidden = w_out.shape[2], w_down.shape[1]
+    shard, section, chunk = rows // nt, width // nz, cols // nz
+    params = jnp.concatenate(
+        [
+            jnp.concatenate([s_uv[0], jnp.pad(s_qk, ((0, 0), (0, hidden - cols))), jnp.zeros((5, hidden), F32)], axis=0),
+            jnp.pad(alpha[0], ((0, 6), (0, 0))),
+        ],
+        axis=1,
+    )
+    steps = jnp.arange(cols, dtype=jnp.int32) % (HEAD_DIM // 2)
+    rates = (10000.0 ** (-steps.astype(F32) / (HEAD_DIM // 2)))[None, :]
+    scratch = buffers(nt, nz, rows, width, cols, hidden, shard, section, chunk)
+    anywhere = pl.BlockSpec(memory_space=pl.ANY)
+    vmem = pl.BlockSpec(memory_space=pltpu.VMEM)
+    smem = pl.BlockSpec(memory_space=pltpu.SMEM)
+    outs = pl.pallas_call(
+        functools.partial(fused_kernel, tuple(scratch), nt, nz),
+        out_shape=(
+            jax.ShapeDtypeStruct((MICRO, rows, cols), BF16),
+            jax.ShapeDtypeStruct((MICRO, rows, cols), BF16),
+            jax.ShapeDtypeStruct((3, section, cols), F32),
+            jax.ShapeDtypeStruct((chunk, width), F32),
+            jax.ShapeDtypeStruct((section * 2 * hidden // 128, 128), F32),
+            jax.ShapeDtypeStruct((hidden // nz, width), F32),
+            jax.ShapeDtypeStruct((1, chunk), F32),
+            jax.ShapeDtypeStruct((2, hidden // nz), F32),
+            jax.ShapeDtypeStruct((2, chunk), F32),
+        ),
+        in_specs=[anywhere, anywhere, smem, anywhere, anywhere, anywhere, anywhere, vmem, vmem],
+        out_specs=(anywhere, anywhere) + (vmem,) * 7,
+        scratch_shapes=list(scratch.values()),
+        compiler_params=pltpu.CompilerParams(
+            collective_id=0, has_side_effects=True, vmem_limit_bytes=60 * 2**20
+        ),
+    )(
+        hidden_in,
+        cotangent,
+        lengths,
+        jnp.transpose(w_qkv[0], (1, 0, 2)),
+        w_out[0],
+        jnp.transpose(w_ug[0], (1, 0, 2)),
+        w_down[0],
+        params,
+        rates,
+    )
+    lo, ig, gq, go, gu, gd, gsqk, gsuv, gal = outs
+    gu = gu.reshape(section, hidden // 128, 2, 128).transpose(0, 2, 1, 3).reshape(section, 2, hidden)
+    return (
+        lo[None],
+        ig[None],
+        jnp.transpose(gq, (1, 0, 2))[None],
+        go[None],
+        gu[None],
+        gd[None],
+        gsqk,
+        gsuv[None],
+        gal[None],
+    )
+
+
 def solution(mesh):
     placed = (
         P(None, "dp", "tensor"),
@@ -511,8 +1209,9 @@
         P("section", None, "tensor"),
         P("section", None, "tensor"),
     )
+    per_rank = per_device_fused if mesh.shape["dp"] == 2 * MICRO and mesh.shape["tensor"] == 4 else per_device
     return jax.shard_map(
-        per_device,
+        per_rank,
         mesh=mesh,
         in_specs=placed,
         out_specs=(

time: 1300 us -> 181 us (0.14); the launches traced: 1280 us -> 179 us
  waiting for transfers between devices: 519 us -> 0 us
  blocking collectives: 326 us -> 0 us
  Pallas kernels: 0 us -> 159 us
  other arithmetic: 119 us -> 1.94 us
  matrix products: 98.2 us -> 0 us
  local copies, waits for them, and re-layouts: 107 us -> 17 us
  starting transfers between devices: 53.5 us -> 0 us
  loops' own time: 38.8 us -> 0 us
  between operations: 23.1 us -> 0.67 us
    reduce_scatter x15 -> x0, waiting for transfers between devices: 341 us -> none  [the longest x6 134 us: to_cols(): lax.psum_scatter(partial_sum.astype(jnp.bfloat16), 'tensor', scatter_dime...]
    psum x23 -> x0, blocking collectives: 205 us -> none  [row_total(): return lax.psum(jnp.sum(values, axis=1), 'tensor')]
    pallas_call x0 -> x1, Pallas kernels: none -> 159 us  [per_device_fused(): pl.pallas_call(functools.partial(fused_kernel, tuple(scratch), nt, nz), o...]
    unnamed x21 -> x0, waiting for transfers between devices: 155 us -> none
    all_gather x12 -> x0, blocking collectives: 111 us -> none  [the longest x6 55.7 us: full_rows(): return lax.all_gather(columns, 'tensor', axis=1, tiled=True)]
    dot_general x105 -> x0, matrix products: 98.2 us -> none  [the longest x12 21.9 us: contract_cols(): lax.dot_general(left_op, right_op, (((1,), (1,)), ((), ())), preferred_el...]
    ppermute x25 -> x0, starting transfers between devices: 52.5 us -> none  [the longest x16 39.8 us: from_behind(): return lax.ppermute(array, axis, pairs)]
    reduce_sum x60 -> x0, other arithmetic: 40.4 us -> none  [the longest x17 16.9 us: row_total(): return lax.psum(jnp.sum(values, axis=1), 'tensor')]
  transfers between devices with their start and end apart: 43 -> 0, of which waited for: 30 -> 0; matrix products, arithmetic and copies ran while one was open for 8% -> 0% of each run, Pallas kernels for 0% -> 0%
where the time goes in v1:
time: 181 us; the launch traced here: 179 us
  Pallas kernels  159 us (88%)
  local copies, waits for them, and re-layouts  17 us (9%)
  other arithmetic  1.94 us (1%)
    pallas_call x1, Pallas kernels, per_device_fused(): pl.pallas_call(functools.partial(fused_kernel, tuple(scratch), nt, nz), o...  159 us
    unnamed x20, local copies, waits for them, and re-layouts  17 us

profile of v1, /device:TPU:8, one launch (start us, length us, event | category | flops | bytes accessed | tf_op | source)
XLA Modules:
  0.0 179.1 jit_solution(5073557066156750671)
XLA Ops:
  0.6 0.6 fusion.6.refs_8_
  1.2 1.4 select_maximum_fusion.refs_7_
  2.6 5.4 %copy.22 = bf16[1,1024,2,1024]{3,1,2,0:T(8,128)(2,1)} copy(bf16[1,1024,2,1024]{3,2,1,0:T(2,128)(2,1)} %param.15) | data formatting | bytes 8388608 | tf_op args[5]
  8.0 159.4 %shard_map.169 = (bf16[2,128,256]{2,1,0:T(8,128)(2,1)}, bf16[2,128,256]{2,1,0:T(8,128)(2,1)}, f32[3,256,256]{2,1,0:T(8,128)}, f32[64,1024]{1,0:T(8,128)}, f32[40...) custom-call(bf16[2,128,256]{2,1,0:T(8,128)(2,1)} %refs_0_.1, ...), custom_call_target="tpu_custom_call" | custom-call | tf_op jit(solution)/shard_map/pallas_call | solution.py:1154
  167.5 0.0 copy-start
  167.5 1.7 copy.32
  169.2 1.6 copy.33
  170.8 2.1 %copy.34 = f32[1,256,3,256]{3,1,2,0:T(8,128)} copy(f32[1,256,3,256]{3,1,2,0:T(8,128)} %bitcast.31) | data formatting | bytes 1572864
  172.8 1.7 copy.35
  174.5 0.0 copy-done
  174.5 0.0 copy-start.1
  174.5 1.3 copy.36
  175.8 0.6 copy-done.1
  176.5 0.0 copy-start.4
  176.5 0.0 copy-start.2
  176.5 0.0 copy-start.3
  176.5 1.0 copy.37
  177.4 0.0 copy-done.4
  177.4 0.5 copy.38
  177.9 0.0 copy-done.2
  177.9 0.6 copy.39
  178.5 0.0 copy-done.3
  178.5 0.6 copy.40
  (1 shorter events, 0.0 us)
Async XLA Ops:
  167.5 7.0 %copy-start = (f32[4096,128]{1,0:T(8,128)S(1)}, f32[4096,128]{1,0:T(8,128)}, u32[]{:S(2)}) copy-start(f32[4096,128]{1,0:T(8,128)} %get-tuple-element.22) | copy-start | bytes 6291460
  174.5 2.0 %copy-start.1 = (f32[256,1024]{1,0:T(8,128)S(1)}, f32[256,1024]{1,0:T(8,128)}, u32[]{:S(2)}) copy-start(f32[256,1024]{1,0:T(8,128)} %get-tuple-element.23) | copy-start | bytes 3145732
  176.5 1.0 copy-start.4
  176.5 1.5 copy-start.2
  176.5 2.1 %copy-start.3 = (f32[2,64]{1,0:T(2,128)S(1)}, f32[2,64]{1,0:T(2,128)}, u32[]{:S(2)}) copy-start(f32[2,64]{1,0:T(2,128)} %get-tuple-element.26) | copy-start | bytes 1540

commit v2 on v1

--- a/solution.py
+++ b/solution.py
@@ -4,6 +4,7 @@
 
 import jax
 import jax.numpy as jnp
+import numpy as np
 from jax import lax
 from jax.experimental import pallas as pl
 from jax.experimental.pallas import tpu as pltpu
@@ -538,11 +539,14 @@
         wo=vmem((2, cols, width), BF16),
         wu=vmem((2, 2, width, hidden), BF16),
         wd=vmem((2, hidden, width), BF16),
-        par=vmem((2, 8, hidden), F32),
-        alp=vmem((2, 8, width), F32),
+        sqk=vmem((2, 1, cols), F32),
+        suv=vmem((2, 2, hidden), F32),
+        alp=vmem((2, 2, width), F32),
+        raw=vmem((2 * hidden // 128 * width, 128), BF16),
+        raw_f=vmem((2 * hidden // 128 * 64, 128), F32),
         full_in=vmem((2, rows, width), BF16),
-        mid_full=vmem((2, rows, width), BF16),
-        dml_full=vmem((2, rows, width), BF16),
+        mid_full=vmem((2, nt, shard, width), BF16),
+        dml_full=vmem((2, nt, shard, width), BF16),
         dat_full=vmem((2, rows, width), BF16),
         fi_p=vmem((rows, width), BF16),
         at_p=vmem((rows, cols), BF16),
@@ -591,7 +595,7 @@
         suv_b=vmem((2, hidden), F32),
         acc=vmem((2, section, hidden), F32),
         w_l=dma((2, 4)), w_rs=dma((4,)),
-        par_l=dma((2,)), par_s=dma((1,)),
+        par_l=dma((2, 2)), par_s=dma((2,)),
         alp_r=dma((2, nt)), alp_s=dma((2, nt)),
         hid_r=dma((nt,)), hid_s=dma((2, nt)),
         cot_r=dma((nt,)), cot_s=dma((2, nt)),
@@ -601,7 +605,7 @@
         rs_ss=dma((8, nt - 1)), rs_rr=dma((8, nt - 1)),
         xa_r=dma((nz, 2)), xa_ss=dma((2, nz)),
         da_r=dma((nz, 2)), da_ss=dma((2, nz)),
-        xf_ss=dma((nt - 1,)), xf_rr=dma((nt - 1,)), df_ss=dma((nt - 1,)), df_rr=dma((nt - 1,)),
+        df_ss=dma((nz - 1, nt - 1)), df_rr=dma((nz - 1, nt - 1)),
         lo_ss=dma((2, nt)), lo_r=dma((2, nt)),
         ig_ss=dma((2, nt)), ig_r=dma((2, nt)),
         al_ss=dma((2, nt - 1)), al_rr=dma((2, nt - 1)),
@@ -612,9 +616,9 @@
 
 
 def fused_kernel(names, nt, nz, *refs):
-    hid, cot, lens, wq_in, wo_in, wu_in, wd_in, par_in, rates = refs[:9]
-    lo, ig, gq, go, gu, gd, gsqk, gsuv, gal = refs[9:18]
-    b = types.SimpleNamespace(**dict(zip(names, refs[18:])))
+    hid, cot, lens, wq_in, wo_in, wu_in, wd_in, sqk_in, suv_in, alp_in, rates = refs[:11]
+    lo, ig, gq, go, gu, gd, gsqk, gsuv, gal = refs[11:20]
+    b = types.SimpleNamespace(**dict(zip(names, refs[20:])))
     rows, width = b.full_in.shape[1:]
     cols, hidden = b.qb.shape[2], b.wd.shape[1]
     shard = b.mid.shape[1]
@@ -641,10 +645,15 @@
     def lanes(index, size):
         return pl.ds(pl.multiple_of(index * size, size), size)
 
-    weights = [(wq_in, b.wq), (wo_in, b.wo), (wu_in, b.wu), (wd_in, b.wd)]
-    for i, (src, dst) in enumerate(weights):
+    weights = [(wq_in, b.wq), (wo_in, b.wo), (None, b.wu), (wd_in, b.wd)]
+    raw_copy = pltpu.make_async_copy(wu_in, b.raw, b.w_l.at[s, 2])
+    raw_copy.start()
+    for i in (0, 1, 3):
+        src, dst = weights[i]
         pltpu.make_async_copy(src, dst.at[s], b.w_l.at[s, i]).start()
-    pltpu.make_async_copy(par_in.at[:, pl.ds(0, hidden)], b.par.at[s], b.par_l.at[s]).start()
+    params = [(sqk_in, b.sqk), (suv_in, b.suv)]
+    for i, (src, dst) in enumerate(params):
+        pltpu.make_async_copy(src, dst.at[s], b.par_l.at[s, i]).start()
 
     barrier = pltpu.get_barrier_semaphore()
     greeted = 0
@@ -660,50 +669,6 @@
             device = (lax.rem(s + dc, 2), t, lax.rem(base + dz, nz))
             pl.semaphore_signal(barrier, inc=1, device_id=device, device_id_type=MESH)
             greeted += 1
-    pl.semaphore_wait(barrier, greeted)
-
-    is_source = s == p
-    for src, rs, ss in ((hid, b.hid_r, b.hid_s), (cot, b.cot_r, b.cot_s)):
-        for dz in range(2):
-            to_mb = lax.rem(p + dz, 2)
-            for dt in range(nt):
-                to_t = around(dt)
-                if src is hid:
-                    piece, place = src.at[to_mb], b.full_in.at[0, :, lanes(t, cols)]
-                else:
-                    piece = src.at[to_mb, pl.ds(pl.multiple_of(to_t * shard, shard), shard), :]
-                    place = b.cot_rows.at[:, lanes(t, cols)]
-                if dz == 0 and dt == 0:
-
-                    @pl.when(is_source)
-                    def _(piece=piece, place=place, rs=rs):
-                        pltpu.make_async_copy(piece, place, rs.at[0]).start()
-                else:
-                    copy = remote(piece, place, ss.at[dz, dt], rs.at[dt], (s, to_t, base + to_mb))
-                    pl.when(is_source)(copy.start)
-                    later(copy, is_source)
-        if src is hid:
-            copy = remote(par_in.at[:, pl.ds(0, hidden)], b.par.at[s], b.par_s.at[0], b.par_l.at[s], peer)
-            copy.start()
-            later(copy)
-            alp_src, alp_dst = par_in.at[:, pl.ds(hidden, cols)], b.alp.at[s, :, lanes(t, cols)]
-            for dc in range(2):
-                for dt in range(nt):
-                    if dc == 0 and dt == 0:
-                        pltpu.make_async_copy(alp_src, alp_dst, b.alp_r.at[s, 0]).start()
-                    else:
-                        copy = remote(alp_src, alp_dst, b.alp_s.at[dc, dt], b.alp_r.at[s, dt], (lax.rem(s + dc, 2), around(dt), z))
-                        copy.start()
-                        later(copy)
-            for i, (src_w, dst_w) in enumerate(weights):
-                copy = remote(src_w, dst_w.at[s], b.w_rs.at[i], b.w_l.at[s, i], peer)
-                copy.start()
-                later(copy)
-
-    def wait_weight(layer, i):
-        src_w, dst_w = weights[i]
-        pltpu.make_async_copy(src_w, dst_w.at[layer], b.w_l.at[layer, i]).wait()
-
     token0 = (base // 2) * pair
     pos_q = token0 + s * rows + lax.broadcasted_iota(jnp.int32, (rows, 1), 0)
     pos_k = token0 + lax.broadcasted_iota(jnp.int32, (1, pair), 1)
@@ -735,6 +700,85 @@
     b.al_s[...] = jnp.zeros_like(b.al_s)
     b.small[...] = jnp.zeros_like(b.small)
 
+    @pl.when(s == 0)
+    def _():
+        b.kv[:, rows:pair, :] = jnp.zeros((2, rows, 2 * cols), BF16)
+
+    @pl.when(s == 1)
+    def _():
+        b.dkv_r[...] = jnp.zeros_like(b.dkv_r)
+
+
+    def to_order():
+        raw_copy.wait()
+        lines = 2 * hidden // 128
+
+        def in_order(step, carry):
+            b.raw_f[...] = b.raw[pl.ds(pl.multiple_of(step * lines * 64, lines * 64), lines * 64), :].astype(F32)
+            at = pl.ds(pl.multiple_of(step * 64, 64), 64)
+            for n in range(hidden // 128):
+                for i in range(2):
+                    b.wu[s, i, at, n * 128 : (n + 1) * 128] = b.raw_f[pl.ds(2 * n + i, 64, stride=lines), :].astype(BF16)
+            return carry
+
+        lax.fori_loop(0, width // 64, in_order, 0)
+
+    pl.semaphore_wait(barrier, greeted)
+    pl.when(s == 1)(to_order)
+
+    is_source = s == p
+    for src, rs, ss in ((hid, b.hid_r, b.hid_s), (cot, b.cot_r, b.cot_s)):
+        for dz in range(2):
+            to_mb = lax.rem(p + dz, 2)
+            for dt in range(nt):
+                to_t = around(dt)
+                if src is hid:
+                    piece, place = src.at[to_mb], b.full_in.at[0, :, lanes(t, cols)]
+                else:
+                    piece = src.at[to_mb, pl.ds(pl.multiple_of(to_t * shard, shard), shard), :]
+                    place = b.cot_rows.at[:, lanes(t, cols)]
+                if dz == 0 and dt == 0:
+
+                    @pl.when(is_source)
+                    def _(piece=piece, place=place, rs=rs):
+                        pltpu.make_async_copy(piece, place, rs.at[0]).start()
+                else:
+                    copy = remote(piece, place, ss.at[dz, dt], rs.at[dt], (s, to_t, base + to_mb))
+                    pl.when(is_source)(copy.start)
+                    later(copy, is_source)
+        if src is hid:
+            for i, (src_p, dst_p) in enumerate(params):
+                copy = remote(src_p, dst_p.at[s], b.par_s.at[i], b.par_l.at[s, i], peer)
+                copy.start()
+                later(copy)
+            alp_src, alp_dst = alp_in, b.alp.at[s, :, lanes(t, cols)]
+            for dc in range(2):
+                for dt in range(nt):
+                    if dc == 0 and dt == 0:
+                        pltpu.make_async_copy(alp_src, alp_dst, b.alp_r.at[s, 0]).start()
+                    else:
+                        copy = remote(alp_src, alp_dst, b.alp_s.at[dc, dt], b.alp_r.at[s, dt], (lax.rem(s + dc, 2), around(dt), z))
+                        copy.start()
+                        later(copy)
+            for i in (0, 1, 3):
+                src_w, dst_w = weights[i]
+                copy = remote(src_w, dst_w.at[s], b.w_rs.at[i], b.w_l.at[s, i], peer)
+                copy.start()
+                later(copy)
+
+    def wait_weight(layer, i):
+        dst_w = weights[i][1].at[layer]
+        wait = pltpu.make_async_copy(dst_w, dst_w, b.w_l.at[layer, i]).wait
+        if i == 2:
+            pl.when(s != layer)(wait)
+        else:
+            wait()
+
+    pl.when(s == 0)(to_order)
+    copy = remote(b.wu.at[s], b.wu.at[s], b.w_rs.at[2], b.w_l.at[s, 2], peer)
+    copy.start()
+    later(copy)
+
     def partner_cols(x):
         half = HEAD_DIM // 2
         return jnp.where(lower, -pltpu.roll(x, cols - half, 1), pltpu.roll(x, half, 1))
@@ -744,8 +788,11 @@
         low = (x - high.astype(F32)).astype(BF16)
         return mul(high, b.blk[...]) + mul(low, b.blk[...])
 
+    def shard_of(ref, index):
+        return ref.at[index] if len(ref.shape) == 3 else ref.at[pl.ds(pl.multiple_of(index * shard, shard), shard), :]
+
     def gather(stage, ref):
-        mine = ref.at[pl.ds(pl.multiple_of(t * shard, shard), shard), :]
+        mine = shard_of(ref, t)
         for k in range(1, nt):
             copy = remote(mine, mine, b.ag_ss.at[stage, k - 1], b.ag_rr.at[stage, k - 1], (s, around(k), z))
             copy.start()
@@ -753,7 +800,7 @@
 
     def gather_wait(stage, ref):
         for k in range(1, nt):
-            theirs = ref.at[pl.ds(pl.multiple_of(around(nt - k) * shard, shard), shard), :]
+            theirs = shard_of(ref, around(nt - k))
             remote(theirs, theirs, b.ag_ss.at[stage, k - 1], b.ag_rr.at[stage, k - 1], (s, around(k), z)).wait_recv()
 
     def scatter(stage):
@@ -774,10 +821,10 @@
     slot = pl.ds(pl.multiple_of((z * 2 + s) * shard, shard), shard)
 
     def my_rows(ref):
-        return ref.at[pl.ds(pl.multiple_of(t * shard, shard), shard), :]
-
-    def to_owner(layer, ref, place_of, send_sems, recv_sems):
-        for k in range(nz):
+        return shard_of(ref, t)
+
+    def to_owner(layer, ref, place_of, send_sems, recv_sems, hops=range(nz)):
+        for k in hops:
             copy = remote(ref, place_of, send_sems.at[layer, k], recv_sems.at[k, s], (layer, t, along(k)))
             if k == 0:
 
@@ -791,19 +838,23 @@
                 copy.start()
                 later(copy)
 
-    def bundle(layer, ref, recv_sems, fwd_ss, fwd_rr):
-        @pl.when(s == layer)
-        def _():
-            for k in range(nz):
+    def bundle(layer, hops):
+        for k in hops:
+            from_z = along(nz - k)
+            rows_of = pl.ds(pl.multiple_of(from_z * 2 * shard, 2 * shard), 2 * shard)
+
+            @pl.when(s == layer)
+            def _(k=k, from_z=from_z):
                 for core in range(2):
-                    row = pl.multiple_of((along(nz - k) * 2 + core) * shard, shard)
-                    place = ref.at[t, pl.ds(row, shard), :]
-                    pltpu.make_async_copy(place, place, recv_sems.at[k, core]).wait()
-
-        for k in range(1, nt):
-            copy = remote(ref.at[t], ref.at[t], fwd_ss.at[k - 1], fwd_rr.at[k - 1], (s, around(k), z))
-            pl.when(s == layer)(copy.start)
-            later(copy, s == layer)
+                    row = pl.multiple_of((from_z * 2 + core) * shard, shard)
+                    place = b.da.at[t, pl.ds(row, shard), :]
+                    pltpu.make_async_copy(place, place, b.da_r.at[k, core]).wait()
+
+            for to in range(1, nt):
+                place = b.da.at[t, rows_of, :]
+                copy = remote(place, place, b.df_ss.at[k - 1, to - 1], b.df_rr.at[k - 1, to - 1], (s, around(to), z))
+                pl.when(s == layer)(copy.start)
+                later(copy, s == layer)
 
     def to_output(layer, ref, out, send_sems, recv_sems):
         to_z = base + s
@@ -833,17 +884,17 @@
                 place = b.full_in.at[0, :, lanes(around(nt - dt), cols)]
                 pltpu.make_async_copy(hid.at[0], place, b.hid_r.at[dt]).wait()
             for src_core in range(2):
-                pltpu.make_async_copy(par_in.at[:, pl.ds(0, hidden)], b.par.at[src_core], b.par_l.at[src_core]).wait()
+                for i, (src_p, dst_p) in enumerate(params):
+                    pltpu.make_async_copy(src_p, dst_p.at[src_core], b.par_l.at[src_core, i]).wait()
                 for dt in range(nt):
                     place = b.alp.at[src_core, :, lanes(around(nt - dt), cols)]
-                    pltpu.make_async_copy(par_in.at[:, pl.ds(hidden, cols)], place, b.alp_r.at[src_core, dt]).wait()
+                    pltpu.make_async_copy(alp_in, place, b.alp_r.at[src_core, dt]).wait()
         else:
             gather_wait(6, full_in)
-            bundle(0, b.xa, b.xa_r, b.xf_ss, b.xf_rr)
         copy = remote(full_in, b.fi_p, b.fi_rs.at[0], b.fi_rs.at[1], peer)
         pl.when(s != layer)(copy.start)
         later(copy, s != layer)
-        scale_qk = b.par[layer, 2:3, 0:cols]
+        scale_qk = b.sqk[layer]
         wait_weight(layer, 0)
         x = full_in[...]
         own = pl.ds(pl.multiple_of(s * rows, rows), rows)
@@ -861,9 +912,9 @@
         b.kv[layer, own, cols : 2 * cols] = mul(x, b.wq[layer, 2]).astype(BF16)
         mine = b.kv.at[layer, own, :]
         copy = remote(mine, mine, b.kv_rs.at[layer, 0], b.kv_rs.at[layer, 1], peer)
-        copy.start()
-        later(copy)
-        copy.wait_recv()
+        pl.when(s == 0)(copy.start)
+        later(copy, s == 0)
+        pl.when(s == 1)(copy.wait_recv)
         att = jnp.zeros((rows, cols), F32)
         for h in range(heads):
             q_h = (b.qb[layer].astype(F32) * picks[h]).astype(BF16)
@@ -890,19 +941,19 @@
         mid_full = b.mid_full.at[layer]
         my_rows(mid_full)[...] = mid.astype(BF16)
         gather(layer, mid_full)
-        to_owner(layer, my_rows(mid_full), b.xa.at[t, slot, :], b.xa_ss, b.xa_r)
         wait_weight(layer, 2)
         wait_weight(layer, 3)
         gather_wait(layer, mid_full)
-        x = mid_full[...]
+        to_owner(layer, mid_full, b.xa.at[:, slot, :], b.xa_ss, b.xa_r)
+        x = mid_full[...].reshape(rows, width)
         for n in range(0, hidden, tile):
             cut = slice(n, n + tile)
             up = mul(x, b.wu[layer, 0, :, cut])
             gate = mul(x, b.wu[layer, 1, :, cut])
             b.up[layer, :, cut] = up
             b.gate[layer, :, cut] = gate
-            gate_s = gate * b.par[layer, 1:2, cut]
-            b.act[:, cut] = (up * b.par[layer, 0:1, cut] * (gate_s / (1.0 + jnp.exp(-gate_s)))).astype(BF16)
+            gate_s = gate * b.suv[layer, 1:2, cut]
+            b.act[:, cut] = (up * b.suv[layer, 0:1, cut] * (gate_s / (1.0 + jnp.exp(-gate_s)))).astype(BF16)
         for n in range(0, width, tile):
             b.rs_s[2 + layer, :, n : n + tile] = mul(b.act[...], b.wd[layer, :, n : n + tile]).astype(BF16)
         scatter(2 + layer)
@@ -916,6 +967,50 @@
             gather(6, b.full_in.at[1])
         to_output(layer, b.out_s.at[layer], lo, b.lo_ss, b.lo_r)
 
+    mine_cols = lanes(z, section_rows)
+
+    def block(k, suv_now):
+        at = lax.rem(t + nt - k, nt)
+        first = suv_now is None
+        if first:
+            for hop in range(nz):
+                for core in range(2):
+                    rows_of = pl.ds(pl.multiple_of((along(nz - hop) * 2 + core) * shard, shard), shard)
+                    for ref, sems in ((b.xa, b.xa_r), (b.da, b.da_r)):
+                        if ref is b.xa or hop == 0:
+                            place = ref.at[:, rows_of, :]
+                            pltpu.make_async_copy(place, place, sems.at[hop, core]).wait()
+        else:
+            for hop in range(1, nz):
+                place = b.da.at[at, pl.ds(pl.multiple_of(along(nz - hop) * 2 * shard, 2 * shard), 2 * shard), :]
+                remote(place, place, b.df_ss.at[hop - 1, k - 1], b.df_rr.at[hop - 1, k - 1], peer).wait_recv()
+
+        def add(ref, value):
+            ref[...] = value if first else ref[...] + value
+
+        new = []
+        for n in range(0, hidden, tile):
+            cut = slice(n, n + tile)
+            up = mul(b.xa[at], b.wu[s, 0, :, cut])
+            gate = mul(b.xa[at], b.wu[s, 1, :, cut])
+            d_act = contract_cols(b.da[at], b.wd[s, cut, :])
+            scale_up, scale_gate = b.suv[s, 0:1, cut], b.suv[s, 1:2, cut]
+            up_s = up * scale_up
+            gate_s = gate * scale_gate
+            sig = 1.0 / (1.0 + jnp.exp(-gate_s))
+            b.act_b[:, cut] = (up_s * gate_s * sig).astype(BF16)
+            d_up = d_act * gate_s * sig
+            d_gate = d_act * up_s * sig * (1.0 + gate_s * (1.0 - sig))
+            new.append((jnp.sum(d_up * up, axis=0, keepdims=True), jnp.sum(d_gate * gate, axis=0, keepdims=True)))
+            x_cut = b.xa[at, :, mine_cols]
+            add(b.acc.at[0, :, cut], contract_rows(x_cut, (d_up * scale_up).astype(BF16)))
+            add(b.acc.at[1, :, cut], contract_rows(x_cut, (d_gate * scale_gate).astype(BF16)))
+        for n in range(0, width, tile):
+            cut = slice(n, n + tile)
+            add(gd.at[:, cut], contract_rows(b.act_b[:, lanes(z, hidden // nz)], b.da[at, :, cut]))
+        sums = tuple(jnp.concatenate([pair_of[i] for pair_of in new], axis=1) for i in range(2))
+        return sums if first else tuple(now + more for now, more in zip(suv_now, sums))
+
     for dt in range(nt):
         place = b.cot_rows.at[:, lanes(around(nt - dt), cols)]
         pltpu.make_async_copy(cot.at[0, pl.ds(0, shard), :], place, b.cot_r.at[dt]).wait()
@@ -925,7 +1020,7 @@
         other = pl.ds(pl.multiple_of((1 - s) * rows, rows), rows)
         rate_a = b.alp[layer, 0:1, :]
         rate_m = b.alp[layer, 1:2, :]
-        scale_qk = b.par[layer, 2:3, 0:cols]
+        scale_qk = b.sqk[layer]
         mid = b.mid[layer]
         mraw_n, ratio_m = ball(b.mraw[layer], width)
         ratio_two = ball(b.ztwo[layer], width)[1]
@@ -935,15 +1030,16 @@
         dml_full = b.dml_full.at[layer]
         my_rows(dml_full)[...] = ball_back(b.mraw[layer], ratio_m, rate_m * d_two, width).astype(BF16)
         gather(2 + layer, dml_full)
-        to_owner(layer, my_rows(dml_full), b.da.at[t, slot, :], b.da_ss, b.da_r)
+        to_owner(layer, my_rows(dml_full), b.da.at[t, slot, :], b.da_ss, b.da_r, range(1, nz))
         gather_wait(2 + layer, dml_full)
-        if layer == 1:
-            bundle(1, b.xa, b.xa_r, b.xf_ss, b.xf_rr)
-        x = dml_full[...]
+        to_owner(layer, dml_full, b.da.at[:, slot, :], b.da_ss, b.da_r, (0,))
+        if layer == 0:
+            bundle(1, (3,))
+        x = dml_full[...].reshape(rows, width)
         for n in range(0, hidden, tile):
             cut = slice(n, n + tile)
             d_act = contract_cols(x, b.wd[layer, cut, :])
-            scale_up, scale_gate = b.par[layer, 0:1, cut], b.par[layer, 1:2, cut]
+            scale_up, scale_gate = b.suv[layer, 0:1, cut], b.suv[layer, 1:2, cut]
             up_s = b.up[layer, :, cut] * scale_up
             gate_s = b.gate[layer, :, cut] * scale_gate
             sig = 1.0 / (1.0 + jnp.exp(-gate_s))
@@ -968,7 +1064,7 @@
             copy.start()
             later(copy)
         gather_wait(4 + layer, dat_full)
-        bundle(layer, b.da, b.da_r, b.df_ss, b.df_rr)
+        bundle(layer, (1, 2))
         for src_v, dst_v, sems in ((dat_full, b.da_p, b.dap_rs), (b.at.at[layer], b.at_p, b.at_rs)):
             copy = remote(src_v, dst_v, sems.at[0], sems.at[1], peer)
             pl.when(s != layer)(copy.start)
@@ -990,14 +1086,28 @@
         b.dkv_f[:, cols : 2 * cols] = dv
         b.dkv_s[layer] = b.dkv_f[other, :].astype(BF16)
         copy = remote(b.dkv_s.at[layer], b.dkv_r.at[layer], b.dkv_rs.at[layer, 0], b.dkv_rs.at[layer, 1], peer)
-        copy.start()
-        later(copy)
+        pl.when(s == 1)(copy.start)
+        later(copy, s == 1)
+
+        @pl.when(s == layer)
+        def _(layer=layer):
+            for dst_v, sems in ((b.da_p, b.dap_rs), (b.at_p, b.at_rs)):
+                remote(dst_v, dst_v, sems.at[0], sems.at[1], peer).wait_recv()
+            for n in range(0, width, tile):
+                cut = slice(n, n + tile)
+                part = contract_rows(b.at[layer], b.dat_full[layer, :, cut]) + contract_rows(b.at_p[...], b.da_p[:, cut])
+                b.wo_f[:, cut] = part
+                b.wo_s[:, cut] = part.astype(BF16)
+            for k in range(1, nz):
+                piece = b.wo_s.at[pl.ds(pl.multiple_of(along(k) * chunk, chunk), chunk), :]
+                remote(piece, b.wo_r.at[k - 1], b.wo_ss.at[k - 1], b.wo_rr.at[k - 1], (layer, t, along(k))).start()
+
         d_scale = jnp.zeros((1, cols), F32)
         for i in range(2):
             if i == 0:
                 grad_n = dq * (1.0 / math.sqrt(HEAD_DIM))
             else:
-                copy.wait_recv()
+                pl.when(s == 0)(copy.wait_recv)
                 grad_n = b.dkv_f[own, 0:cols] + b.dkv_r[layer, :, 0:cols].astype(F32)
             rotated, ratio = b.rot[layer, i], b.rat[layer, i]
             d_scale = d_scale + jnp.sum(grad_n * rotated * ratio, axis=0, keepdims=True)
@@ -1027,7 +1137,7 @@
 
         @pl.when(s == layer)
         def _(layer=layer):
-            for dst_v, sems in ((b.fi_p, b.fi_rs), (b.da_p, b.dap_rs), (b.at_p, b.at_rs), (b.dq_p, b.dq_rs)):
+            for dst_v, sems in ((b.fi_p, b.fi_rs), (b.dq_p, b.dq_rs)):
                 remote(dst_v, dst_v, sems.at[0], sems.at[1], peer).wait_recv()
             for k in (1, 2, 3, 0):
                 cut = lanes(along(k), section_rows)
@@ -1038,57 +1148,16 @@
                 else:
                     for i in range(3):
                         gq[i] = part[:, i * cols : (i + 1) * cols]
-            for n in range(0, width, tile):
-                cut = slice(n, n + tile)
-                part = contract_rows(b.at[layer], b.dat_full[layer, :, cut]) + contract_rows(b.at_p[...], b.da_p[:, cut])
-                b.wo_f[:, cut] = part
-                b.wo_s[:, cut] = part.astype(BF16)
-            for k in range(1, nz):
-                piece = b.wo_s.at[pl.ds(pl.multiple_of(along(k) * chunk, chunk), chunk), :]
-                remote(piece, b.wo_r.at[k - 1], b.wo_ss.at[k - 1], b.wo_rr.at[k - 1], (layer, t, along(k))).start()
-
+
+        if layer == 0:
+            bundle(0, (3,))
+            suv = block(0, None)
         d_hin = (1.0 - rate_a) * d_one + scatter_wait(6 + layer)
         b.ig_s[layer] = d_hin.astype(BF16)
         to_output(layer, b.ig_s.at[layer], ig, b.ig_ss, b.ig_r)
         grad_out = b.ig_s[layer].astype(F32)
 
-    mine_cols = lanes(z, section_rows)
-    for ref in (b.acc, gd, gsuv):
-        ref[...] = jnp.zeros_like(ref)
-    suv_total = jnp.zeros((2, hidden), F32)
-
-    def block(k, suv_now):
-        at = lax.rem(t + nt - k, nt)
-
-        @pl.when(k > 0)
-        def _():
-            for ref, ss, rr in ((b.xa, b.xf_ss, b.xf_rr), (b.da, b.df_ss, b.df_rr)):
-                remote(ref.at[at], ref.at[at], ss.at[k - 1], rr.at[k - 1], peer).wait_recv()
-
-        new = []
-        for n in range(0, hidden, tile):
-            cut = slice(n, n + tile)
-            up = mul(b.xa[at], b.wu[s, 0, :, cut])
-            gate = mul(b.xa[at], b.wu[s, 1, :, cut])
-            d_act = contract_cols(b.da[at], b.wd[s, cut, :])
-            scale_up, scale_gate = b.par[s, 0:1, cut], b.par[s, 1:2, cut]
-            up_s = up * scale_up
-            gate_s = gate * scale_gate
-            sig = 1.0 / (1.0 + jnp.exp(-gate_s))
-            b.act_b[:, cut] = (up_s * gate_s * sig).astype(BF16)
-            d_up = d_act * gate_s * sig
-            d_gate = d_act * up_s * sig * (1.0 + gate_s * (1.0 - sig))
-            new.append((jnp.sum(d_up * up, axis=0, keepdims=True), jnp.sum(d_gate * gate, axis=0, keepdims=True)))
-            x_cut = b.xa[at, :, mine_cols]
-            b.acc[0, :, cut] += contract_rows(x_cut, (d_up * scale_up).astype(BF16))
-            b.acc[1, :, cut] += contract_rows(x_cut, (d_gate * scale_gate).astype(BF16))
-        for n in range(0, width, tile):
-            gd[:, n : n + tile] += contract_rows(b.act_b[:, lanes(z, hidden // nz)], b.da[at, :, n : n + tile])
-        return tuple(
-            jnp.concatenate([pair_of[i] for pair_of in new], axis=1) + suv_now[i] for i in range(2)
-        )
-
-    suv = lax.fori_loop(0, nt, block, (suv_total[0:1], suv_total[1:2]))
+    suv = lax.fori_loop(1, nt, block, suv)
     for i in range(2):
         b.suv_b[i : i + 1, :] = suv[i]
     gsuv[...] = b.suv_b[:, lanes(z, hidden // nz)]
@@ -1133,20 +1202,28 @@
             pl.when(when)(copy.wait_send)
 
 
+def copy_kernel(*refs):
+    count = len(refs) // 3
+    sems = refs[-1]
+    reads = [pltpu.make_async_copy(refs[i], refs[2 * count + i], sems.at[0, i]) for i in range(count)]
+    writes = [pltpu.make_async_copy(refs[2 * count + i], refs[count + i], sems.at[1, i]) for i in range(count)]
+    for copy in reads:
+        copy.start()
+    for read, write in zip(reads, writes):
+        read.wait()
+        write.start()
+    for copy in writes:
+        copy.wait()
+
+
 def per_device_fused(hidden_in, cotangent, lengths, w_qkv, w_out, w_ug, w_down, s_qk, s_uv, alpha):
     nt, nz = lax.axis_size("tensor"), lax.axis_size("dp")
     rows, cols = hidden_in.shape[1:]
     width, hidden = w_out.shape[2], w_down.shape[1]
     shard, section, chunk = rows // nt, width // nz, cols // nz
-    params = jnp.concatenate(
-        [
-            jnp.concatenate([s_uv[0], jnp.pad(s_qk, ((0, 0), (0, hidden - cols))), jnp.zeros((5, hidden), F32)], axis=0),
-            jnp.pad(alpha[0], ((0, 6), (0, 0))),
-        ],
-        axis=1,
-    )
-    steps = jnp.arange(cols, dtype=jnp.int32) % (HEAD_DIM // 2)
-    rates = (10000.0 ** (-steps.astype(F32) / (HEAD_DIM // 2)))[None, :]
+    half = HEAD_DIM // 2
+    rates = (10000.0 ** (-(np.arange(cols) % half).astype(np.float32) / half)).astype(np.float32)[None, :]
+    pairs = w_ug[0].reshape(width, 2, hidden // 128, 128).transpose(0, 2, 1, 3).reshape(2 * hidden // 128 * width, 128)
     scratch = buffers(nt, nz, rows, width, cols, hidden, shard, section, chunk)
     anywhere = pl.BlockSpec(memory_space=pl.ANY)
     vmem = pl.BlockSpec(memory_space=pltpu.VMEM)
@@ -1164,7 +1241,7 @@
             jax.ShapeDtypeStruct((2, hidden // nz), F32),
             jax.ShapeDtypeStruct((2, chunk), F32),
         ),
-        in_specs=[anywhere, anywhere, smem, anywhere, anywhere, anywhere, anywhere, vmem, vmem],
+        in_specs=[anywhere, anywhere, smem] + [anywhere] * 7 + [vmem],
         out_specs=(anywhere, anywhere) + (vmem,) * 7,
         scratch_shapes=list(scratch.values()),
         compiler_params=pltpu.CompilerParams(
@@ -1176,12 +1253,21 @@
         lengths,
         jnp.transpose(w_qkv[0], (1, 0, 2)),
         w_out[0],
-        jnp.transpose(w_ug[0], (1, 0, 2)),
+        pairs,
         w_down[0],
-        params,
-        rates,
+        s_qk,
+        s_uv[0],
+        alpha[0],
+        jnp.asarray(rates),
     )
-    lo, ig, gq, go, gu, gd, gsqk, gsuv, gal = outs
+    lo, ig, gq, go, gu, gd, gsqk, gsuv, gal = pl.pallas_call(
+        copy_kernel,
+        out_shape=tuple(jax.ShapeDtypeStruct(o.shape, o.dtype) for o in outs),
+        in_specs=[anywhere] * len(outs),
+        out_specs=(anywhere,) * len(outs),
+        scratch_shapes=[pltpu.VMEM(o.shape, o.dtype) for o in outs] + [pltpu.SemaphoreType.DMA((2, len(outs)))],
+        compiler_params=pltpu.CompilerParams(vmem_limit_bytes=60 * 2**20),
+    )(*outs)
     gu = gu.reshape(section, hidden // 128, 2, 128).transpose(0, 2, 1, 3).reshape(section, 2, hidden)
     return (
         lo[None],

time: 181 us -> 147 us (0.81)
  local copies, waits for them, and re-layouts: 17 us -> 0 us
  Pallas kernels: 159 us -> 146 us
  other arithmetic: 1.94 us -> 0 us
    pallas_call x1, Pallas kernels: 159 us -> 142 us  [per_device_fused(): pl.pallas_call(functools.partial(fused_kernel, tuple(scratch), nt, nz), o...]
    unnamed x20 -> x0, local copies, waits for them, and re-layouts: 17 us -> none
    pallas_call x0 -> x1, Pallas kernels: none -> 3.99 us  [per_device_fused(): pl.pallas_call(copy_kernel, out_shape=tuple((jax.ShapeDtypeStruct(o.shape...]
where the time goes in v2:
time: 147 us
  Pallas kernels  146 us (99%)
    pallas_call x1, Pallas kernels, per_device_fused(): pl.pallas_call(functools.partial(fused_kernel, tuple(scratch), nt, nz), o...  142 us
    pallas_call x1, Pallas kernels, per_device_fused(): pl.pallas_call(copy_kernel, out_shape=tuple((jax.ShapeDtypeStruct(o.shape...  3.99 us

profile of v2, /device:TPU:8, one launch (start us, length us, event | category | flops | bytes accessed | tf_op | source)
XLA Modules:
  0.0 146.6 jit_solution(12539436942761245442)
XLA Ops:
  0.6 141.8 %shard_map.178 = (bf16[2,128,256]{2,1,0:T(8,128)(2,1)}, bf16[2,128,256]{2,1,0:T(8,128)(2,1)}, f32[3,256,256]{2,1,0:T(8,128)}, f32[64,1024]{1,0:T(8,128)}, f32[40...) custom-call(bf16[2,128,256]{2,1,0:T(8,128)(2,1)} %refs_0_.1, ...), custom_call_target="tpu_custom_call" | custom-call | tf_op jit(solution)/shard_map/pallas_call | solution.py:1231
  142.5 4.0 %shard_map.179 = (bf16[2,128,256]{2,1,0:T(8,128)(2,1)}, bf16[2,128,256]{2,1,0:T(8,128)(2,1)}, f32[3,256,256]{2,1,0:T(8,128)}, f32[64,1024]{1,0:T(8,128)}, f32[40...) custom-call(bf16[2,128,256]{2,1,0:T(8,128)(2,1)} %get-tuple-element.27.refs_0_, ...), custom_call_target="tpu_custom_call" | custom-call | tf_op jit(solution)/shard_map/pallas_call | solution.py:1263

commit v3 on v2

--- a/solution.py
+++ b/solution.py
@@ -606,6 +606,7 @@
         xa_r=dma((nz, 2)), xa_ss=dma((2, nz)),
         da_r=dma((nz, 2)), da_ss=dma((2, nz)),
         df_ss=dma((nz - 1, nt - 1)), df_rr=dma((nz - 1, nt - 1)),
+        xf_ss=dma((nz - 1, nt - 1)), xf_rr=dma((nz - 1, nt - 1)),
         lo_ss=dma((2, nt)), lo_r=dma((2, nt)),
         ig_ss=dma((2, nt)), ig_r=dma((2, nt)),
         al_ss=dma((2, nt - 1)), al_rr=dma((2, nt - 1)),
@@ -634,7 +635,9 @@
     pending = []
 
     def around(k):
-        return lax.rem(t + k, nt)
+        return lax.rem(lax.div(t, 2) + k // 2, 2) * 2 + lax.rem(lax.rem(t, 2) + k % 2, 2)
+
+    peers = (3, 1, 2)
 
     def along(k):
         return lax.rem(z + k, nz)
@@ -724,13 +727,12 @@
         lax.fori_loop(0, width // 64, in_order, 0)
 
     pl.semaphore_wait(barrier, greeted)
-    pl.when(s == 1)(to_order)
 
     is_source = s == p
     for src, rs, ss in ((hid, b.hid_r, b.hid_s), (cot, b.cot_r, b.cot_s)):
         for dz in range(2):
             to_mb = lax.rem(p + dz, 2)
-            for dt in range(nt):
+            for dt in peers + (0,):
                 to_t = around(dt)
                 if src is hid:
                     piece, place = src.at[to_mb], b.full_in.at[0, :, lanes(t, cols)]
@@ -774,7 +776,7 @@
         else:
             wait()
 
-    pl.when(s == 0)(to_order)
+    to_order()
     copy = remote(b.wu.at[s], b.wu.at[s], b.w_rs.at[2], b.w_l.at[s, 2], peer)
     copy.start()
     later(copy)
@@ -793,18 +795,18 @@
 
     def gather(stage, ref):
         mine = shard_of(ref, t)
-        for k in range(1, nt):
+        for k in peers:
             copy = remote(mine, mine, b.ag_ss.at[stage, k - 1], b.ag_rr.at[stage, k - 1], (s, around(k), z))
             copy.start()
             later(copy)
 
     def gather_wait(stage, ref):
         for k in range(1, nt):
-            theirs = shard_of(ref, around(nt - k))
+            theirs = shard_of(ref, around(k))
             remote(theirs, theirs, b.ag_ss.at[stage, k - 1], b.ag_rr.at[stage, k - 1], (s, around(k), z)).wait_recv()
 
     def scatter(stage):
-        for k in range(1, nt):
+        for k in peers:
             piece = b.rs_s.at[stage, pl.ds(pl.multiple_of(around(k) * shard, shard), shard), :]
             copy = remote(piece, b.rs_r.at[stage, k - 1], b.rs_ss.at[stage, k - 1], b.rs_rr.at[stage, k - 1], (s, around(k), z))
             copy.start()
@@ -838,7 +840,11 @@
                 copy.start()
                 later(copy)
 
-    def bundle(layer, hops):
+    x_rows = (b.xa, b.xa_r, b.xf_ss, b.xf_rr)
+    d_rows = (b.da, b.da_r, b.df_ss, b.df_rr)
+
+    def bundle(layer, hops, group):
+        ref, arrived, send_sems, recv_sems = group
         for k in hops:
             from_z = along(nz - k)
             rows_of = pl.ds(pl.multiple_of(from_z * 2 * shard, 2 * shard), 2 * shard)
@@ -847,12 +853,12 @@
             def _(k=k, from_z=from_z):
                 for core in range(2):
                     row = pl.multiple_of((from_z * 2 + core) * shard, shard)
-                    place = b.da.at[t, pl.ds(row, shard), :]
-                    pltpu.make_async_copy(place, place, b.da_r.at[k, core]).wait()
+                    place = ref.at[t, pl.ds(row, shard), :]
+                    pltpu.make_async_copy(place, place, arrived.at[k, core]).wait()
 
             for to in range(1, nt):
-                place = b.da.at[t, rows_of, :]
-                copy = remote(place, place, b.df_ss.at[k - 1, to - 1], b.df_rr.at[k - 1, to - 1], (s, around(to), z))
+                place = ref.at[t, rows_of, :]
+                copy = remote(place, place, send_sems.at[k - 1, to - 1], recv_sems.at[k - 1, to - 1], (s, around(to), z))
                 pl.when(s == layer)(copy.start)
                 later(copy, s == layer)
 
@@ -881,13 +887,13 @@
         full_in = b.full_in.at[layer]
         if layer == 0:
             for dt in range(nt):
-                place = b.full_in.at[0, :, lanes(around(nt - dt), cols)]
+                place = b.full_in.at[0, :, lanes(around(dt), cols)]
                 pltpu.make_async_copy(hid.at[0], place, b.hid_r.at[dt]).wait()
             for src_core in range(2):
                 for i, (src_p, dst_p) in enumerate(params):
                     pltpu.make_async_copy(src_p, dst_p.at[src_core], b.par_l.at[src_core, i]).wait()
                 for dt in range(nt):
-                    place = b.alp.at[src_core, :, lanes(around(nt - dt), cols)]
+                    place = b.alp.at[src_core, :, lanes(around(dt), cols)]
                     pltpu.make_async_copy(alp_in, place, b.alp_r.at[src_core, dt]).wait()
         else:
             gather_wait(6, full_in)
@@ -941,10 +947,12 @@
         mid_full = b.mid_full.at[layer]
         my_rows(mid_full)[...] = mid.astype(BF16)
         gather(layer, mid_full)
+        if layer == 1:
+            to_owner(1, my_rows(mid_full), b.xa.at[t, slot, :], b.xa_ss, b.xa_r, range(1, nz))
         wait_weight(layer, 2)
         wait_weight(layer, 3)
         gather_wait(layer, mid_full)
-        to_owner(layer, mid_full, b.xa.at[:, slot, :], b.xa_ss, b.xa_r)
+        to_owner(layer, mid_full, b.xa.at[:, slot, :], b.xa_ss, b.xa_r, range(nz) if layer == 0 else (0,))
         x = mid_full[...].reshape(rows, width)
         for n in range(0, hidden, tile):
             cut = slice(n, n + tile)
@@ -957,6 +965,8 @@
         for n in range(0, width, tile):
             b.rs_s[2 + layer, :, n : n + tile] = mul(b.act[...], b.wd[layer, :, n : n + tile]).astype(BF16)
         scatter(2 + layer)
+        if layer == 1:
+            bundle(1, (1,), x_rows)
         mraw = scatter_wait(2 + layer)
         b.mraw[layer] = mraw
         ztwo = mid + rate_m * (ball(mraw, width)[0] - mid)
@@ -970,20 +980,28 @@
     mine_cols = lanes(z, section_rows)
 
     def block(k, suv_now):
-        at = lax.rem(t + nt - k, nt)
+        at = lax.rem(lax.div(t, 2) + lax.div(k, 2), 2) * 2 + lax.rem(t + k, 2)
         first = suv_now is None
         if first:
             for hop in range(nz):
                 for core in range(2):
                     rows_of = pl.ds(pl.multiple_of((along(nz - hop) * 2 + core) * shard, shard), shard)
                     for ref, sems in ((b.xa, b.xa_r), (b.da, b.da_r)):
-                        if ref is b.xa or hop == 0:
-                            place = ref.at[:, rows_of, :]
-                            pltpu.make_async_copy(place, place, sems.at[hop, core]).wait()
+                        place = ref.at[:, rows_of, :]
+                        wait = pltpu.make_async_copy(place, place, sems.at[hop, core]).wait
+                        if hop == 0:
+                            wait()
+                        elif ref is b.xa:
+                            pl.when(s == 0)(wait)
         else:
             for hop in range(1, nz):
-                place = b.da.at[at, pl.ds(pl.multiple_of(along(nz - hop) * 2 * shard, 2 * shard), 2 * shard), :]
-                remote(place, place, b.df_ss.at[hop - 1, k - 1], b.df_rr.at[hop - 1, k - 1], peer).wait_recv()
+                for ref, _, ss, rr in (d_rows, x_rows):
+                    place = ref.at[at, pl.ds(pl.multiple_of(along(nz - hop) * 2 * shard, 2 * shard), 2 * shard), :]
+                    wait = remote(place, place, ss.at[hop - 1, k - 1], rr.at[hop - 1, k - 1], peer).wait_recv
+                    if ref is b.da:
+                        wait()
+                    else:
+                        pl.when(s == 1)(wait)
 
         def add(ref, value):
             ref[...] = value if first else ref[...] + value
@@ -1012,7 +1030,7 @@
         return sums if first else tuple(now + more for now, more in zip(suv_now, sums))
 
     for dt in range(nt):
-        place = b.cot_rows.at[:, lanes(around(nt - dt), cols)]
+        place = b.cot_rows.at[:, lanes(around(dt), cols)]
         pltpu.make_async_copy(cot.at[0, pl.ds(0, shard), :], place, b.cot_r.at[dt]).wait()
     grad_out = b.cot_rows[...].astype(F32)
     for layer in (1, 0):
@@ -1031,10 +1049,12 @@
         my_rows(dml_full)[...] = ball_back(b.mraw[layer], ratio_m, rate_m * d_two, width).astype(BF16)
         gather(2 + layer, dml_full)
         to_owner(layer, my_rows(dml_full), b.da.at[t, slot, :], b.da_ss, b.da_r, range(1, nz))
+        if layer == 1:
+            bundle(1, (2, 3), x_rows)
         gather_wait(2 + layer, dml_full)
         to_owner(layer, dml_full, b.da.at[:, slot, :], b.da_ss, b.da_r, (0,))
         if layer == 0:
-            bundle(1, (3,))
+            bundle(1, (3,), d_rows)
         x = dml_full[...].reshape(rows, width)
         for n in range(0, hidden, tile):
             cut = slice(n, n + tile)
@@ -1064,7 +1084,6 @@
             copy.start()
             later(copy)
         gather_wait(4 + layer, dat_full)
-        bundle(layer, (1, 2))
         for src_v, dst_v, sems in ((dat_full, b.da_p, b.dap_rs), (b.at.at[layer], b.at_p, b.at_rs)):
             copy = remote(src_v, dst_v, sems.at[0], sems.at[1], peer)
             pl.when(s != layer)(copy.start)
@@ -1082,6 +1101,7 @@
             dv = dv + contract_rows(prob.astype(BF16), d_att_h)
             dq = dq + picks[h] * mul(d_score, b.kv[layer, :, 0:cols])
             dk = dk + contract_rows(d_score, q_h)
+        bundle(layer, (1, 2), d_rows)
         b.dkv_f[:, 0:cols] = dk * (1.0 / math.sqrt(HEAD_DIM))
         b.dkv_f[:, cols : 2 * cols] = dv
         b.dkv_s[layer] = b.dkv_f[other, :].astype(BF16)
@@ -1150,7 +1170,7 @@
                         gq[i] = part[:, i * cols : (i + 1) * cols]
 
         if layer == 0:
-            bundle(0, (3,))
+            bundle(0, (3,), d_rows)
             suv = block(0, None)
         d_hin = (1.0 - rate_a) * d_one + scatter_wait(6 + layer)
         b.ig_s[layer] = d_hin.astype(BF16)
@@ -1189,7 +1209,7 @@
     for out, sems in ((lo, b.lo_r), (ig, b.ig_r)):
         for m in range(2):
             for k in range(nt):
-                place = out.at[m, pl.ds(pl.multiple_of(around(nt - k) * shard, shard), shard), :]
+                place = out.at[m, pl.ds(pl.multiple_of(around(k) * shard, shard), shard), :]
                 pltpu.make_async_copy(place, place, sems.at[m, k]).wait()
     for k in range(nz - 1):
         remote(b.wq_s.at[k], b.wq_r.at[k], b.wq_ss.at[k], b.wq_rr.at[k], peer).wait_send()

time: 147 us -> 140 us (0.952)
  Pallas kernels: 146 us -> 139 us
    pallas_call x1, Pallas kernels: 142 us -> 135 us  [per_device_fused(): pl.pallas_call(functools.partial(fused_kernel, tuple(scratch), nt, nz), o...]
where the time goes in v3:
time: 140 us
  Pallas kernels  139 us (99%)
    pallas_call x1, Pallas kernels, per_device_fused(): pl.pallas_call(functools.partial(fused_kernel, tuple(scratch), nt, nz), o...  135 us
    pallas_call x1, Pallas kernels, per_device_fused(): pl.pallas_call(copy_kernel, out_shape=tuple((jax.ShapeDtypeStruct(o.shape...  3.99 us

profile of v3, /device:TPU:8, one launch (start us, length us, event | category | flops | bytes accessed | tf_op | source)
XLA Modules:
  0.0 139.7 jit_solution(5509434895180293247)
XLA Ops:
  0.6 134.9 %shard_map.178 = (bf16[2,128,256]{2,1,0:T(8,128)(2,1)}, bf16[2,128,256]{2,1,0:T(8,128)(2,1)}, f32[3,256,256]{2,1,0:T(8,128)}, f32[64,1024]{1,0:T(8,128)}, f32[40...) custom-call(bf16[2,128,256]{2,1,0:T(8,128)(2,1)} %refs_0_.1, ...), custom_call_target="tpu_custom_call" | custom-call | tf_op jit(solution)/shard_map/pallas_call | solution.py:1251
  135.5 4.0 %shard_map.179 = (bf16[2,128,256]{2,1,0:T(8,128)(2,1)}, bf16[2,128,256]{2,1,0:T(8,128)(2,1)}, f32[3,256,256]{2,1,0:T(8,128)}, f32[64,1024]{1,0:T(8,128)}, f32[40...) custom-call(bf16[2,128,256]{2,1,0:T(8,128)(2,1)} %get-tuple-element.27.refs_0_, ...), custom_call_target="tpu_custom_call" | custom-call | tf_op jit(solution)/shard_map/pallas_call | solution.py:1283

commit v4 on v3

--- a/solution.py
+++ b/solution.py
@@ -587,7 +587,7 @@
         small=vmem((2, 8, cols), F32),
         sm_r=vmem((nz, 2, 8, cols), F32),
         wq_s=vmem((nz - 1, section, 3 * cols), BF16),
-        wq_r=vmem((nz - 1, section, 3 * cols), BF16),
+        wq_r=vmem((nz, section, 3 * cols), BF16),
         wo_f=vmem((cols, width), F32),
         wo_s=vmem((cols, width), BF16),
         wo_r=vmem((nz - 1, chunk, width), BF16),
@@ -602,7 +602,7 @@
         fi_rs=dma((2,)), at_rs=dma((2,)), dap_rs=dma((2,)), dq_rs=dma((2,)),
         kv_rs=dma((2, 2)), dkv_rs=dma((2, 2)),
         ag_ss=dma((7, nt - 1)), ag_rr=dma((7, nt - 1)),
-        rs_ss=dma((8, nt - 1)), rs_rr=dma((8, nt - 1)),
+        rs_ss=dma((8, 2, nt - 1)), rs_rr=dma((8, 2, nt - 1)),
         xa_r=dma((nz, 2)), xa_ss=dma((2, nz)),
         da_r=dma((nz, 2)), da_ss=dma((2, nz)),
         df_ss=dma((nz - 1, nt - 1)), df_rr=dma((nz - 1, nt - 1)),
@@ -611,7 +611,7 @@
         ig_ss=dma((2, nt)), ig_r=dma((2, nt)),
         al_ss=dma((2, nt - 1)), al_rr=dma((2, nt - 1)),
         sm_ss=dma((2, nz)), sm_rr=dma((nz, 2)),
-        wq_ss=dma((nz - 1,)), wq_rr=dma((nz - 1,)),
+        wq_ss=dma((nz - 1,)), wq_rr=dma((nz,)),
         wo_ss=dma((nz - 1,)), wo_rr=dma((nz - 1,)),
     )
 
@@ -805,19 +805,22 @@
             theirs = shard_of(ref, around(k))
             remote(theirs, theirs, b.ag_ss.at[stage, k - 1], b.ag_rr.at[stage, k - 1], (s, around(k), z)).wait_recv()
 
-    def scatter(stage):
+    def scatter(stage, n):
+        cut = pl.ds(n * tile, tile)
         for k in peers:
-            piece = b.rs_s.at[stage, pl.ds(pl.multiple_of(around(k) * shard, shard), shard), :]
-            copy = remote(piece, b.rs_r.at[stage, k - 1], b.rs_ss.at[stage, k - 1], b.rs_rr.at[stage, k - 1], (s, around(k), z))
+            piece = b.rs_s.at[stage, pl.ds(pl.multiple_of(around(k) * shard, shard), shard), cut]
+            copy = remote(piece, b.rs_r.at[stage, k - 1, :, cut], b.rs_ss.at[stage, n, k - 1], b.rs_rr.at[stage, n, k - 1], (s, around(k), z))
             copy.start()
             later(copy)
 
     def scatter_wait(stage):
         total = b.rs_s[stage, pl.ds(pl.multiple_of(t * shard, shard), shard), :].astype(F32)
+        for n in range(width // tile):
+            for k in range(1, nt):
+                place = b.rs_r.at[stage, k - 1, :, pl.ds(n * tile, tile)]
+                remote(place, place, b.rs_ss.at[stage, n, k - 1], b.rs_rr.at[stage, n, k - 1], (s, around(k), z)).wait_recv()
         for k in range(1, nt):
-            place = b.rs_r.at[stage, k - 1]
-            remote(place, place, b.rs_ss.at[stage, k - 1], b.rs_rr.at[stage, k - 1], (s, around(k), z)).wait_recv()
-            total = total + place[...].astype(F32)
+            total = total + b.rs_r[stage, k - 1].astype(F32)
         return total
 
     slot = pl.ds(pl.multiple_of((z * 2 + s) * shard, shard), shard)
@@ -882,6 +885,19 @@
             else:
                 copy.start()
                 later(copy)
+
+    upper = z // 2
+    end, hub = 3 * upper, 1 + upper
+    sibling = end + hub - z
+    far_end, far_hub = 3 - end, 3 - hub
+
+    def hub_step(layer, n):
+        @pl.when((s == layer) & (z == hub))
+        def _():
+            remote(b.wq_s.at[n], b.wq_r.at[n], b.wq_ss.at[n], b.wq_rr.at[n], peer).wait_recv()
+            b.wq_s[n] = (b.wq_s[n].astype(F32) + b.wq_r[n].astype(F32)).astype(BF16)
+            to_z = far_hub if n else far_end
+            remote(b.wq_s.at[n], b.wq_r.at[3], b.wq_ss.at[n], b.wq_rr.at[3], (layer, t, to_z)).start()
 
     for layer in range(2):
         full_in = b.full_in.at[layer]
@@ -934,7 +950,7 @@
         wait_weight(layer, 1)
         for n in range(0, width, tile):
             b.rs_s[layer, :, n : n + tile] = mul(b.at[layer], b.wo[layer, :, n : n + tile]).astype(BF16)
-        scatter(layer)
+            scatter(layer, n // tile)
         hin = my_rows(full_in)[...].astype(F32)
         rate_a = b.alp[layer, 0:1, :]
         rate_m = b.alp[layer, 1:2, :]
@@ -964,7 +980,7 @@
             b.act[:, cut] = (up * b.suv[layer, 0:1, cut] * (gate_s / (1.0 + jnp.exp(-gate_s)))).astype(BF16)
         for n in range(0, width, tile):
             b.rs_s[2 + layer, :, n : n + tile] = mul(b.act[...], b.wd[layer, :, n : n + tile]).astype(BF16)
-        scatter(2 + layer)
+            scatter(2 + layer, n // tile)
         if layer == 1:
             bundle(1, (1,), x_rows)
         mraw = scatter_wait(2 + layer)
@@ -1069,7 +1085,7 @@
             cut = slice(n, n + tile)
             part = contract_cols(b.duv[0], b.wu[layer, 0, cut, :]) + contract_cols(b.duv[1], b.wu[layer, 1, cut, :])
             b.rs_s[4 + layer, :, cut] = part.astype(BF16)
-        scatter(4 + layer)
+            scatter(4 + layer, n // tile)
         hin = my_rows(b.full_in.at[layer])[...].astype(F32)
         araw_n, ratio_a = ball(b.araw[layer], width)
         ratio_one = ball(b.zone[layer], width)[1]
@@ -1083,6 +1099,9 @@
             copy = remote(b.al_s.at[layer, :, lanes(around(k), cols)], b.al_r.at[layer, k - 1], b.al_ss.at[layer, k - 1], b.al_rr.at[layer, k - 1], (s, around(k), z))
             copy.start()
             later(copy)
+        if layer == 0:
+            hub_step(1, 0)
+            hub_step(1, 1)
         gather_wait(4 + layer, dat_full)
         for src_v, dst_v, sems in ((dat_full, b.da_p, b.dap_rs), (b.at.at[layer], b.at_p, b.at_rs)):
             copy = remote(src_v, dst_v, sems.at[0], sems.at[1], peer)
@@ -1137,15 +1156,15 @@
             b.dqkv[layer, :, i * cols : (i + 1) * cols] = d_raw.astype(BF16)
         d_val = b.dkv_f[own, cols : 2 * cols] + b.dkv_r[layer, :, cols : 2 * cols].astype(F32)
         b.dqkv[layer, :, 2 * cols : 3 * cols] = d_val.astype(BF16)
+        copy = remote(b.dqkv.at[layer], b.dq_p, b.dq_rs.at[0], b.dq_rs.at[1], peer)
+        pl.when(s != layer)(copy.start)
+        later(copy, s != layer)
         for n in range(0, width, tile):
             part = contract_cols(b.dqkv[layer, :, 0:cols], b.wq[layer, 0, n : n + tile, :])
             for i in range(1, 3):
                 part = part + contract_cols(b.dqkv[layer, :, i * cols : (i + 1) * cols], b.wq[layer, i, n : n + tile, :])
             b.rs_s[6 + layer, :, n : n + tile] = part.astype(BF16)
-        scatter(6 + layer)
-        copy = remote(b.dqkv.at[layer], b.dq_p, b.dq_rs.at[0], b.dq_rs.at[1], peer)
-        pl.when(s != layer)(copy.start)
-        later(copy, s != layer)
+            scatter(6 + layer, n // tile)
         total = b.al_s[layer, :, lanes(t, cols)]
         for k in range(1, nt):
             place = b.al_r.at[layer, k - 1]
@@ -1159,25 +1178,32 @@
         def _(layer=layer):
             for dst_v, sems in ((b.fi_p, b.fi_rs), (b.dq_p, b.dq_rs)):
                 remote(dst_v, dst_v, sems.at[0], sems.at[1], peer).wait_recv()
-            for k in (1, 2, 3, 0):
-                cut = lanes(along(k), section_rows)
+            for n, index in enumerate((far_end, far_hub, sibling, z)):
+                cut = lanes(index, section_rows)
                 part = contract_rows(b.full_in[layer, :, cut], b.dqkv[layer]) + contract_rows(b.fi_p[:, cut], b.dq_p[...])
-                if k:
-                    b.wq_s[k - 1] = part.astype(BF16)
-                    remote(b.wq_s.at[k - 1], b.wq_r.at[k - 1], b.wq_ss.at[k - 1], b.wq_rr.at[k - 1], (layer, t, along(k))).start()
-                else:
+                if n == 3:
                     for i in range(3):
                         gq[i] = part[:, i * cols : (i + 1) * cols]
+                    continue
+                b.wq_s[n] = part.astype(BF16)
+                start = remote(b.wq_s.at[n], b.wq_r.at[n], b.wq_ss.at[n], b.wq_rr.at[n], (layer, t, sibling)).start
+                if n == 2:
+                    start()
+                else:
+                    pl.when(z == end)(start)
 
         if layer == 0:
             bundle(0, (3,), d_rows)
             suv = block(0, None)
+            hub_step(0, 0)
         d_hin = (1.0 - rate_a) * d_one + scatter_wait(6 + layer)
         b.ig_s[layer] = d_hin.astype(BF16)
         to_output(layer, b.ig_s.at[layer], ig, b.ig_ss, b.ig_r)
         grad_out = b.ig_s[layer].astype(F32)
 
-    suv = lax.fori_loop(1, nt, block, suv)
+    suv = block(1, suv)
+    hub_step(0, 1)
+    suv = lax.fori_loop(2, nt, block, suv)
     for i in range(2):
         b.suv_b[i : i + 1, :] = suv[i]
     gsuv[...] = b.suv_b[:, lanes(z, hidden // nz)]
@@ -1186,11 +1212,11 @@
         for i in range(2):
             gu[pl.ds(2 * j + i, section_rows, stride=per_row), :] = b.acc[i, :, j * 128 : (j + 1) * 128]
 
-    for k in range(1, nz):
-        place = b.wq_r.at[k - 1]
-        remote(place, place, b.wq_ss.at[k - 1], b.wq_rr.at[k - 1], peer).wait_recv()
+    for n in (2, 3):
+        place = b.wq_r.at[n]
+        remote(place, place, b.wq_ss.at[2], b.wq_rr.at[n], peer).wait_recv()
         for i in range(3):
-            gq[i] += b.wq_r[k - 1, :, i * cols : (i + 1) * cols].astype(F32)
+            gq[i] += b.wq_r[n, :, i * cols : (i + 1) * cols].astype(F32)
     total = b.wo_f[pl.ds(pl.multiple_of(z * chunk, chunk), chunk), :]
     for k in range(1, nz):
         place = b.wo_r.at[k - 1]

time: 140 us -> 135 us (0.964)
  Pallas kernels: 139 us -> 134 us
    pallas_call x1, Pallas kernels: 135 us -> 130 us  [per_device_fused(): pl.pallas_call(functools.partial(fused_kernel, tuple(scratch), nt, nz), o...]
where the time goes in v4:
time: 135 us
  Pallas kernels  134 us (99%)
    pallas_call x1, Pallas kernels, per_device_fused(): pl.pallas_call(functools.partial(fused_kernel, tuple(scratch), nt, nz), o...  130 us
    pallas_call x1, Pallas kernels, per_device_fused(): pl.pallas_call(copy_kernel, out_shape=tuple((jax.ShapeDtypeStruct(o.shape...  3.99 us

profile of v4, /device:TPU:8, one launch (start us, length us, event | category | flops | bytes accessed | tf_op | source)
XLA Modules:
  0.0 134.8 jit_solution(11017103251986461879)
XLA Ops:
  0.6 130.0 %shard_map.178 = (bf16[2,128,256]{2,1,0:T(8,128)(2,1)}, bf16[2,128,256]{2,1,0:T(8,128)(2,1)}, f32[3,256,256]{2,1,0:T(8,128)}, f32[64,1024]{1,0:T(8,128)}, f32[40...) custom-call(bf16[2,128,256]{2,1,0:T(8,128)(2,1)} %refs_0_.1, ...), custom_call_target="tpu_custom_call" | custom-call | tf_op jit(solution)/shard_map/pallas_call | solution.py:1277
  130.6 4.0 %shard_map.179 = (bf16[2,128,256]{2,1,0:T(8,128)(2,1)}, bf16[2,128,256]{2,1,0:T(8,128)(2,1)}, f32[3,256,256]{2,1,0:T(8,128)}, f32[64,1024]{1,0:T(8,128)}, f32[40...) custom-call(bf16[2,128,256]{2,1,0:T(8,128)(2,1)} %get-tuple-element.27.refs_0_, ...), custom_call_target="tpu_custom_call" | custom-call | tf_op jit(solution)/shard_map/pallas_call | solution.py:1309

commit v5 on v4

--- a/solution.py
+++ b/solution.py
@@ -611,7 +611,7 @@
         ig_ss=dma((2, nt)), ig_r=dma((2, nt)),
         al_ss=dma((2, nt - 1)), al_rr=dma((2, nt - 1)),
         sm_ss=dma((2, nz)), sm_rr=dma((nz, 2)),
-        wq_ss=dma((nz - 1,)), wq_rr=dma((nz,)),
+        wq_ss=dma((nz - 1, 2)), wq_rr=dma((nz, 2)),
         wo_ss=dma((nz - 1,)), wo_rr=dma((nz - 1,)),
     )
 
@@ -729,7 +729,7 @@
     pl.semaphore_wait(barrier, greeted)
 
     is_source = s == p
-    for src, rs, ss in ((hid, b.hid_r, b.hid_s), (cot, b.cot_r, b.cot_s)):
+    def spread_rows(src, rs, ss):
         for dz in range(2):
             to_mb = lax.rem(p + dz, 2)
             for dt in peers + (0,):
@@ -748,25 +748,26 @@
                     copy = remote(piece, place, ss.at[dz, dt], rs.at[dt], (s, to_t, base + to_mb))
                     pl.when(is_source)(copy.start)
                     later(copy, is_source)
-        if src is hid:
-            for i, (src_p, dst_p) in enumerate(params):
-                copy = remote(src_p, dst_p.at[s], b.par_s.at[i], b.par_l.at[s, i], peer)
+
+    spread_rows(hid, b.hid_r, b.hid_s)
+    for i, (src_p, dst_p) in enumerate(params):
+        copy = remote(src_p, dst_p.at[s], b.par_s.at[i], b.par_l.at[s, i], peer)
+        copy.start()
+        later(copy)
+    alp_src, alp_dst = alp_in, b.alp.at[s, :, lanes(t, cols)]
+    for dc in range(2):
+        for dt in range(nt):
+            if dc == 0 and dt == 0:
+                pltpu.make_async_copy(alp_src, alp_dst, b.alp_r.at[s, 0]).start()
+            else:
+                copy = remote(alp_src, alp_dst, b.alp_s.at[dc, dt], b.alp_r.at[s, dt], (lax.rem(s + dc, 2), around(dt), z))
                 copy.start()
                 later(copy)
-            alp_src, alp_dst = alp_in, b.alp.at[s, :, lanes(t, cols)]
-            for dc in range(2):
-                for dt in range(nt):
-                    if dc == 0 and dt == 0:
-                        pltpu.make_async_copy(alp_src, alp_dst, b.alp_r.at[s, 0]).start()
-                    else:
-                        copy = remote(alp_src, alp_dst, b.alp_s.at[dc, dt], b.alp_r.at[s, dt], (lax.rem(s + dc, 2), around(dt), z))
-                        copy.start()
-                        later(copy)
-            for i in (0, 1, 3):
-                src_w, dst_w = weights[i]
-                copy = remote(src_w, dst_w.at[s], b.w_rs.at[i], b.w_l.at[s, i], peer)
-                copy.start()
-                later(copy)
+    for i in (0, 1, 3):
+        src_w, dst_w = weights[i]
+        copy = remote(src_w, dst_w.at[s], b.w_rs.at[i], b.w_l.at[s, i], peer)
+        copy.start()
+        later(copy)
 
     def wait_weight(layer, i):
         dst_w = weights[i][1].at[layer]
@@ -891,13 +892,17 @@
     sibling = end + hub - z
     far_end, far_hub = 3 - end, 3 - hub
 
-    def hub_step(layer, n):
+    def qkv_part(n, to, half, device):
+        rows_of = pl.ds(half * (section_rows // 2), section_rows // 2)
+        return remote(b.wq_s.at[n, rows_of], b.wq_r.at[to, rows_of], b.wq_ss.at[n, half], b.wq_rr.at[to, half], device)
+
+    def hub_step(layer, n, half):
         @pl.when((s == layer) & (z == hub))
         def _():
-            remote(b.wq_s.at[n], b.wq_r.at[n], b.wq_ss.at[n], b.wq_rr.at[n], peer).wait_recv()
-            b.wq_s[n] = (b.wq_s[n].astype(F32) + b.wq_r[n].astype(F32)).astype(BF16)
-            to_z = far_hub if n else far_end
-            remote(b.wq_s.at[n], b.wq_r.at[3], b.wq_ss.at[n], b.wq_rr.at[3], (layer, t, to_z)).start()
+            qkv_part(n, n, half, peer).wait_recv()
+            rows_of = pl.ds(half * (section_rows // 2), section_rows // 2)
+            b.wq_s[n, rows_of] = (b.wq_s[n, rows_of].astype(F32) + b.wq_r[n, rows_of].astype(F32)).astype(BF16)
+            qkv_part(n, 3, half, (layer, t, far_hub if n else far_end)).start()
 
     for layer in range(2):
         full_in = b.full_in.at[layer]
@@ -905,6 +910,7 @@
             for dt in range(nt):
                 place = b.full_in.at[0, :, lanes(around(dt), cols)]
                 pltpu.make_async_copy(hid.at[0], place, b.hid_r.at[dt]).wait()
+            spread_rows(cot, b.cot_r, b.cot_s)
             for src_core in range(2):
                 for i, (src_p, dst_p) in enumerate(params):
                     pltpu.make_async_copy(src_p, dst_p.at[src_core], b.par_l.at[src_core, i]).wait()
@@ -920,22 +926,21 @@
         wait_weight(layer, 0)
         x = full_in[...]
         own = pl.ds(pl.multiple_of(s * rows, rows), rows)
-        for i in range(2):
+        def normed_heads(i):
             raw = mul(x, b.wq[layer, i])
             rotated = raw * b.cosb[...] + partner_cols(raw) * b.sinb[...]
             ratio = lax.rsqrt(head_total(rotated * rotated) / HEAD_DIM + EPSILON)
             b.rot[layer, i] = rotated
             b.rat[layer, i] = ratio
-            normed = (rotated * ratio * scale_qk).astype(BF16)
-            if i == 0:
-                b.qb[layer] = normed
-            else:
-                b.kv[layer, own, 0:cols] = normed
+            return (rotated * ratio * scale_qk).astype(BF16)
+
+        b.kv[layer, own, 0:cols] = normed_heads(1)
         b.kv[layer, own, cols : 2 * cols] = mul(x, b.wq[layer, 2]).astype(BF16)
         mine = b.kv.at[layer, own, :]
         copy = remote(mine, mine, b.kv_rs.at[layer, 0], b.kv_rs.at[layer, 1], peer)
         pl.when(s == 0)(copy.start)
         later(copy, s == 0)
+        b.qb[layer] = normed_heads(0)
         pl.when(s == 1)(copy.wait_recv)
         att = jnp.zeros((rows, cols), F32)
         for h in range(heads):
@@ -991,11 +996,11 @@
         if layer == 0:
             my_rows(b.full_in.at[1])[...] = b.out_s[0]
             gather(6, b.full_in.at[1])
-        to_output(layer, b.out_s.at[layer], lo, b.lo_ss, b.lo_r)
+            to_output(0, b.out_s.at[0], lo, b.lo_ss, b.lo_r)
 
     mine_cols = lanes(z, section_rows)
 
-    def block(k, suv_now):
+    def block(k, suv_now, between=None):
         at = lax.rem(lax.div(t, 2) + lax.div(k, 2), 2) * 2 + lax.rem(t + k, 2)
         first = suv_now is None
         if first:
@@ -1036,6 +1041,8 @@
             d_up = d_act * gate_s * sig
             d_gate = d_act * up_s * sig * (1.0 + gate_s * (1.0 - sig))
             new.append((jnp.sum(d_up * up, axis=0, keepdims=True), jnp.sum(d_gate * gate, axis=0, keepdims=True)))
+            if between is not None and n:
+                between()
             x_cut = b.xa[at, :, mine_cols]
             add(b.acc.at[0, :, cut], contract_rows(x_cut, (d_up * scale_up).astype(BF16)))
             add(b.acc.at[1, :, cut], contract_rows(x_cut, (d_gate * scale_gate).astype(BF16)))
@@ -1064,6 +1071,10 @@
         dml_full = b.dml_full.at[layer]
         my_rows(dml_full)[...] = ball_back(b.mraw[layer], ratio_m, rate_m * d_two, width).astype(BF16)
         gather(2 + layer, dml_full)
+        if layer == 1:
+            to_output(1, b.out_s.at[1], lo, b.lo_ss, b.lo_r)
+        else:
+            to_output(1, b.ig_s.at[1], ig, b.ig_ss, b.ig_r)
         to_owner(layer, my_rows(dml_full), b.da.at[t, slot, :], b.da_ss, b.da_r, range(1, nz))
         if layer == 1:
             bundle(1, (2, 3), x_rows)
@@ -1100,15 +1111,16 @@
             copy.start()
             later(copy)
         if layer == 0:
-            hub_step(1, 0)
-            hub_step(1, 1)
+            for n in range(2):
+                for half in range(2):
+                    hub_step(1, n, half)
         gather_wait(4 + layer, dat_full)
         for src_v, dst_v, sems in ((dat_full, b.da_p, b.dap_rs), (b.at.at[layer], b.at_p, b.at_rs)):
             copy = remote(src_v, dst_v, sems.at[0], sems.at[1], peer)
             pl.when(s != layer)(copy.start)
             later(copy, s != layer)
         d_att = contract_cols(dat_full[...], b.wo[layer])
-        dq = jnp.zeros((rows, cols), F32)
+        d_scores = []
         dk = jnp.zeros((pair, cols), F32)
         dv = jnp.zeros((pair, cols), F32)
         for h in range(heads):
@@ -1118,15 +1130,18 @@
             d_prob = contract_cols(d_att_h, b.kv[layer, :, cols : 2 * cols])
             d_score = (prob * (d_prob - jnp.sum(prob * d_prob, axis=1, keepdims=True))).astype(BF16)
             dv = dv + contract_rows(prob.astype(BF16), d_att_h)
-            dq = dq + picks[h] * mul(d_score, b.kv[layer, :, 0:cols])
+            d_scores.append(d_score)
             dk = dk + contract_rows(d_score, q_h)
-        bundle(layer, (1, 2), d_rows)
         b.dkv_f[:, 0:cols] = dk * (1.0 / math.sqrt(HEAD_DIM))
         b.dkv_f[:, cols : 2 * cols] = dv
         b.dkv_s[layer] = b.dkv_f[other, :].astype(BF16)
         copy = remote(b.dkv_s.at[layer], b.dkv_r.at[layer], b.dkv_rs.at[layer, 0], b.dkv_rs.at[layer, 1], peer)
         pl.when(s == 1)(copy.start)
         later(copy, s == 1)
+        bundle(layer, (1, 2), d_rows)
+        dq = jnp.zeros((rows, cols), F32)
+        for h in range(heads):
+            dq = dq + picks[h] * mul(d_scores[h], b.kv[layer, :, 0:cols])
 
         @pl.when(s == layer)
         def _(layer=layer):
@@ -1159,23 +1174,7 @@
         copy = remote(b.dqkv.at[layer], b.dq_p, b.dq_rs.at[0], b.dq_rs.at[1], peer)
         pl.when(s != layer)(copy.start)
         later(copy, s != layer)
-        for n in range(0, width, tile):
-            part = contract_cols(b.dqkv[layer, :, 0:cols], b.wq[layer, 0, n : n + tile, :])
-            for i in range(1, 3):
-                part = part + contract_cols(b.dqkv[layer, :, i * cols : (i + 1) * cols], b.wq[layer, i, n : n + tile, :])
-            b.rs_s[6 + layer, :, n : n + tile] = part.astype(BF16)
-            scatter(6 + layer, n // tile)
-        total = b.al_s[layer, :, lanes(t, cols)]
-        for k in range(1, nt):
-            place = b.al_r.at[layer, k - 1]
-            remote(place, place, b.al_ss.at[layer, k - 1], b.al_rr.at[layer, k - 1], peer).wait_recv()
-            total = total + place[...]
-        b.small[layer] = total
-        b.small[layer, 2:3, :] = d_scale
-        to_owner(layer, b.small.at[layer], b.sm_r.at[lax.rem(z, nz), s], b.sm_ss, b.sm_rr)
-
-        @pl.when(s == layer)
-        def _(layer=layer):
+        def qkv_pieces(layer=layer):
             for dst_v, sems in ((b.fi_p, b.fi_rs), (b.dq_p, b.dq_rs)):
                 remote(dst_v, dst_v, sems.at[0], sems.at[1], peer).wait_recv()
             for n, index in enumerate((far_end, far_hub, sibling, z)):
@@ -1186,23 +1185,48 @@
                         gq[i] = part[:, i * cols : (i + 1) * cols]
                     continue
                 b.wq_s[n] = part.astype(BF16)
-                start = remote(b.wq_s.at[n], b.wq_r.at[n], b.wq_ss.at[n], b.wq_rr.at[n], (layer, t, sibling)).start
-                if n == 2:
-                    start()
-                else:
-                    pl.when(z == end)(start)
+                for half in range(2):
+                    start = qkv_part(n, n, half, (layer, t, sibling)).start
+                    if n == 2:
+                        start()
+                    else:
+                        pl.when(z == end)(start)
+
+        def last_sum(layer=layer):
+            for n in range(0, width, tile):
+                part = contract_cols(b.dqkv[layer, :, 0:cols], b.wq[layer, 0, n : n + tile, :])
+                for i in range(1, 3):
+                    part = part + contract_cols(b.dqkv[layer, :, i * cols : (i + 1) * cols], b.wq[layer, i, n : n + tile, :])
+                b.rs_s[6 + layer, :, n : n + tile] = part.astype(BF16)
+                scatter(6 + layer, n // tile)
+
+        if layer == 1:
+            last_sum()
+        pl.when(s == layer)(qkv_pieces)
+        if layer == 0:
+            last_sum()
+        total = b.al_s[layer, :, lanes(t, cols)]
+        for k in range(1, nt):
+            place = b.al_r.at[layer, k - 1]
+            remote(place, place, b.al_ss.at[layer, k - 1], b.al_rr.at[layer, k - 1], peer).wait_recv()
+            total = total + place[...]
+        b.small[layer] = total
+        b.small[layer, 2:3, :] = d_scale
+        to_owner(layer, b.small.at[layer], b.sm_r.at[lax.rem(z, nz), s], b.sm_ss, b.sm_rr)
 
         if layer == 0:
             bundle(0, (3,), d_rows)
             suv = block(0, None)
-            hub_step(0, 0)
+            hub_step(0, 0, 0)
         d_hin = (1.0 - rate_a) * d_one + scatter_wait(6 + layer)
         b.ig_s[layer] = d_hin.astype(BF16)
-        to_output(layer, b.ig_s.at[layer], ig, b.ig_ss, b.ig_r)
+        if layer == 0:
+            to_output(0, b.ig_s.at[0], ig, b.ig_ss, b.ig_r)
         grad_out = b.ig_s[layer].astype(F32)
 
-    suv = block(1, suv)
-    hub_step(0, 1)
+    hub_step(0, 0, 1)
+    suv = block(1, suv, lambda: hub_step(0, 1, 0))
+    hub_step(0, 1, 1)
     suv = lax.fori_loop(2, nt, block, suv)
     for i in range(2):
         b.suv_b[i : i + 1, :] = suv[i]
@@ -1213,10 +1237,11 @@
             gu[pl.ds(2 * j + i, section_rows, stride=per_row), :] = b.acc[i, :, j * 128 : (j + 1) * 128]
 
     for n in (2, 3):
-        place = b.wq_r.at[n]
-        remote(place, place, b.wq_ss.at[2], b.wq_rr.at[n], peer).wait_recv()
-        for i in range(3):
-            gq[i] += b.wq_r[n, :, i * cols : (i + 1) * cols].astype(F32)
+        for half in range(2):
+            qkv_part(2, n, half, peer).wait_recv()
+            rows_of = slice(half * (section_rows // 2), (half + 1) * (section_rows // 2))
+            for i in range(3):
+                gq[i, rows_of] += b.wq_r[n, rows_of, i * cols : (i + 1) * cols].astype(F32)
     total = b.wo_f[pl.ds(pl.multiple_of(z * chunk, chunk), chunk), :]
     for k in range(1, nz):
         place = b.wo_r.at[k - 1]
@@ -1238,7 +1263,8 @@
                 place = out.at[m, pl.ds(pl.multiple_of(around(k) * shard, shard), shard), :]
                 pltpu.make_async_copy(place, place, sems.at[m, k]).wait()
     for k in range(nz - 1):
-        remote(b.wq_s.at[k], b.wq_r.at[k], b.wq_ss.at[k], b.wq_rr.at[k], peer).wait_send()
+        for half in range(2):
+            qkv_part(k, k, half, peer).wait_send()
         piece = b.wo_s.at[pl.ds(0, chunk), :]
         remote(piece, b.wo_r.at[k], b.wo_ss.at[k], b.wo_rr.at[k], peer).wait_send()
     for copy, when in pending:

time: 135 us -> 134 us (level)
  no operation moved by 1% of the time
where the time goes in v5:
time: 134 us
  Pallas kernels  133 us (99%)
    pallas_call x1, Pallas kernels, per_device_fused(): pl.pallas_call(functools.partial(fused_kernel, tuple(scratch), nt, nz), o...  129 us
    pallas_call x1, Pallas kernels, per_device_fused(): pl.pallas_call(copy_kernel, out_shape=tuple((jax.ShapeDtypeStruct(o.shape...  3.99 us

profile of v5, /device:TPU:8, one launch (start us, length us, event | category | flops | bytes accessed | tf_op | source)
XLA Modules:
  0.0 133.7 jit_solution(11475038896038521012)
XLA Ops:
  0.6 128.8 %shard_map.178 = (bf16[2,128,256]{2,1,0:T(8,128)(2,1)}, bf16[2,128,256]{2,1,0:T(8,128)(2,1)}, f32[3,256,256]{2,1,0:T(8,128)}, f32[64,1024]{1,0:T(8,128)}, f32[40...) custom-call(bf16[2,128,256]{2,1,0:T(8,128)(2,1)} %refs_0_.1, ...), custom_call_target="tpu_custom_call" | custom-call | tf_op jit(solution)/shard_map/pallas_call | solution.py:1303
  129.5 4.0 %shard_map.179 = (bf16[2,128,256]{2,1,0:T(8,128)(2,1)}, bf16[2,128,256]{2,1,0:T(8,128)(2,1)}, f32[3,256,256]{2,1,0:T(8,128)}, f32[64,1024]{1,0:T(8,128)}, f32[40...) custom-call(bf16[2,128,256]{2,1,0:T(8,128)(2,1)} %get-tuple-element.27.refs_0_, ...), custom_call_target="tpu_custom_call" | custom-call | tf_op jit(solution)/shard_map/pallas_call | solution.py:1335
